TPU v7x, 256 devices: a whole 4x4x8 slice. The times are simulated.
256 devices in a mesh: dom: 256 (over x, y, z, core).
Axes of the slice: x: 4, y: 4, z: 8, core: 2. Of those that a mesh axis runs over, the one named last changes fastest.
Arguments:
- entities: float32 [200, 98304], P(None, 'dom'), may hold values from -3 to 3
- entity_state: float32 [98304], P('dom'), may hold values from 0.05 to 1
- relations: float32 [200, 7424], replicated, may hold values from -3 to 3
- relation_state: float32 [7424], replicated, may hold values from 0.05 to 1
- head_rows: int32 [256, 2048], P('dom'), may hold values from 0 to 383
- relation_ids: int32 [256, 2048], P('dom'), may hold values from 0 to 7423
- tail_rows: int32 [256, 2048], P('dom'), may hold values from 0 to 383
- neg_rows: int32 [256, 2, 2, 384], P('dom'), may hold values from 0 to 383
- edge_counts: int32 [256], P('dom'), may hold values from 1 to 2048, 262144 in all
- matching: int32 [256], P('dom'), may hold values from 0 to 255, as said below
Outputs:
- new_entities: float32 [200, 98304], P(None, 'dom')
- new_entity_state: float32 [98304], P('dom')
- new_relations: float32 [200, 7424], replicated
- new_relation_state: float32 [7424], replicated
Inputs may be any that keep to these rules, and one draw needn't show every extreme that they name: matching[b] = b XOR s for one s of 1 to 255 shared by all b, so matching is its own inverse and never fixes a bucket.
All inputs are finite; a program needn't handle non-finite values. No bound on the sum of `edge_counts` on one device may be relied on, other than what follows from the above.
Results may differ from a plain program's by a relative error of at most 0.0003.
Values sent between devices are 32-bit elements; how exact they have to be, the bound alone decides.
No kernel may reach another device: no remote copies, remote signals or barrier semaphores. Data moves between devices by JAX's collectives and lax.ppermute only.
A program may use at most 128 MiB of HBM per device.

v0:
```python
import functools

import jax
import jax.numpy as jnp
from jax import lax
from jax.experimental import pallas as pl
from jax.experimental.pallas import tpu as pltpu
from jax.sharding import PartitionSpec as P

TILE = 128
HALF = 104
PART = 2 * HALF
VMEM_LIMIT = 48 * 2**20
STEP_RATE = 0.3
EPSILON = 1e-08

CORE = (0, 1)
Z = (1, 3)
Y = (4, 2)
X = (6, 2)


def xor_permute(value, mask):
    size = lax.axis_size("dom")
    return lax.ppermute(value, "dom", [(i, i ^ mask) for i in range(size)])


def partner_exchange(value, xor_value, low, width, work, *operands):
    pick = (xor_value >> low) & (2**width - 1)

    def branch(mask, v, *rest):
        moved = xor_permute(v, mask << low) if mask else v
        return moved, work(*rest)

    branches = [functools.partial(branch, mask) for mask in range(2**width)]
    return lax.switch(pick, branches, value, *operands)


def members(axis, cores):
    low, width = axis
    mask = (2**width - 1) << low
    size = lax.axis_size("dom")
    return [
        [base | (k << low) for k in range(2**width)]
        for base in range(size)
        if base & mask == 0 and (base & 1) in cores
    ]


def swap_chunks(value, groups):
    return lax.all_to_all(value, "dom", 0, 0, axis_index_groups=groups, tiled=True)


def scatter_sum(value, groups):
    ways = len(groups[0])
    moved = swap_chunks(value, groups)
    return jnp.sum(moved.reshape((ways, value.shape[0] // ways) + value.shape[1:]), axis=0)


def spread(value, groups):
    ways = len(groups[0])
    copies = jnp.broadcast_to(value[None], (ways,) + value.shape)
    return swap_chunks(copies.reshape((ways * value.shape[0],) + value.shape[1:]), groups)


def update_relations(keep, received, relations, relation_state):
    me = lax.axis_index("dom")
    core, cy, cx = me & 1, (me >> 4) & 3, (me >> 6) & 3
    half, width, _ = keep.shape
    first = members(X, (0,)) + members(Y, (1,))
    second = members(Y, (0,)) + members(X, (1,))
    along_z = members(Z, (0, 1))

    part = keep + received
    part = scatter_sum(part, first)
    part = scatter_sum(part, second)
    owned = part.shape[0]
    flat = part.reshape(owned * width // 8, 8, TILE)
    rows = flat.shape[0]
    flat = jnp.pad(flat, ((0, -rows % 8), (0, 0), (0, 0)))
    flat = spread(scatter_sum(flat, along_z), along_z)
    total = flat[:rows].reshape(owned, width, TILE).transpose(1, 0, 2).reshape(width, owned * TILE)

    outer = jnp.where(core == 0, cx, cy)
    inner = jnp.where(core == 0, cy, cx)
    start = (core * half + outer * (half // 4) + inner * owned) * TILE
    values = lax.dynamic_slice_in_dim(relations, start, owned * TILE, 1)
    state = lax.dynamic_slice_in_dim(relation_state, start, owned * TILE)
    new_state = state + jnp.mean(total * total, axis=0)
    new_values = values - STEP_RATE * total / jnp.sqrt(new_state + EPSILON)[None, :]
    packed = jnp.concatenate([new_values, jnp.broadcast_to(new_state[None], (8, owned * TILE))], axis=0)
    packed = packed.reshape(width + 8, owned, TILE).transpose(1, 0, 2)
    packed = spread(packed, second)
    packed = spread(packed, first)
    other = xor_permute(packed, 1)
    low = jnp.where(core == 0, packed, other)
    high = jnp.where(core == 0, other, packed)
    count = relations.shape[1]
    both = jnp.concatenate([low, high[: count // TILE - half]], axis=0)
    new_relations = both[:, :width].transpose(1, 0, 2).reshape(width, count)
    return new_relations, both[:, width].reshape(count)


def split_parts(x):
    high = x.astype(jnp.bfloat16)
    low = (x - high.astype(jnp.float32)).astype(jnp.bfloat16)
    return high, low


def dot(a, b):
    return jnp.dot(a, b, preferred_element_type=jnp.float32)


def dot_nt(a, b):
    return lax.dot_general(a, b, (((1,), (1,)), ((), ())), preferred_element_type=jnp.float32)


def one_hot(condition):
    return jnp.where(condition, 1.0, 0.0).astype(jnp.bfloat16)


def gather_kernel(first_slot, live_ref, ids_ref, table_ref, out_ref, parts):
    width, count = table_ref.shape
    high, low = split_parts(table_ref[...])
    blank = jnp.zeros((PART - width, count), jnp.bfloat16)
    parts[:PART, :] = jnp.concatenate([high, blank], axis=0)
    parts[PART:, :] = jnp.concatenate([low, blank], axis=0)
    edges = ids_ref.shape[1]
    chunk = 256
    half = width // 2

    @pl.loop(0, edges // chunk)
    def _(c):
        at = pl.ds(pl.multiple_of(c * chunk, chunk), chunk)
        slots = first_slot + c * chunk + lax.broadcasted_iota(jnp.int32, (1, chunk), 1)
        ids = jnp.where(slots < live_ref[0], ids_ref[:, at], -1)
        hot = one_hot(lax.broadcasted_iota(jnp.int32, (count, chunk), 0) == ids)
        cols = dot(parts[...], hot)
        cols = cols[:PART] + cols[PART:]
        out_ref[:HALF, at] = cols[:HALF]
        out_ref[HALF:, at] = cols[half : half + HALF]


def gather_relations(live, ids, relations, first_slot):
    width, count = relations.shape
    edges = ids.shape[1]
    return pl.pallas_call(
        functools.partial(gather_kernel, first_slot),
        out_shape=jax.ShapeDtypeStruct((PART, edges), jnp.float32),
        in_specs=[
            pl.BlockSpec(memory_space=pltpu.SMEM),
            pl.BlockSpec(memory_space=pltpu.VMEM),
            pl.BlockSpec(memory_space=pltpu.VMEM),
        ],
        out_specs=pl.BlockSpec(memory_space=pltpu.VMEM),
        scratch_shapes=[pltpu.VMEM((2 * PART, count), jnp.bfloat16)],
        compiler_params=pltpu.CompilerParams(vmem_limit_bytes=VMEM_LIMIT),
        cost_estimate=pl.CostEstimate(
            flops=4 * PART * count * edges, bytes_accessed=width * count * 4, transcendentals=0
        ),
        name="gather_relations",
    )(live, ids, relations)


def padded_halves(block):
    half = block.shape[0] // 2
    blank = jnp.zeros((HALF - half, block.shape[1]), block.dtype)
    return jnp.concatenate([block[:half], blank, block[half:], blank], axis=0)


def edge_kernel(
    live_ref, heads_ref, tails_ref, negs_ref, head_ref, tail_ref, rels_ref,
    head_grad_ref, tail_grad_ref, rel_grad_ref,
    cols_ref, flip_ref, wide_ref, query_ref, weight_ref, counts_ref, sums_ref,
):
    width, rows = head_ref.shape
    edges = heads_ref.shape[1]
    chunk = weight_ref.shape[1]
    groups = negs_ref.shape[0]
    half = width // 2

    for side, ref in enumerate((head_ref, tail_ref)):
        block = padded_halves(ref[...])
        high, low = split_parts(block)
        cols_ref[side, :PART, :] = high
        cols_ref[side, PART:, :] = low
        wide_ref[side, :, :rows] = high
        wide_ref[side, :, rows : 2 * rows] = high
        wide_ref[side, :, 2 * rows :] = low
        turned = jnp.concatenate([block, jnp.zeros((256 - PART, rows), jnp.float32)], axis=0).T
        high, low = split_parts(turned)
        flip_ref[side, :, :256] = high
        flip_ref[side, :, 256:512] = high
        flip_ref[side, :, 512:] = low
    for group in range(groups):
        for which in range(2):
            hits = lax.broadcasted_iota(jnp.int32, (rows, negs_ref.shape[-1]), 0) == negs_ref[group, which][None, :]
            count = jnp.sum(jnp.where(hits, 1.0 / negs_ref.shape[-1], 0.0), axis=1, keepdims=True)
            counts_ref[group, which] = jnp.broadcast_to(count, (rows, 128))
    query_ref[...] = jnp.zeros_like(query_ref)
    sums_ref[...] = jnp.zeros_like(sums_ref)

    def put_query(side, query):
        high, low = split_parts(query)
        query_ref[side, :PART, :] = high
        query_ref[side, 256 : 256 + PART, :] = low
        query_ref[side, 512 : 512 + PART, :] = high

    def put_weight(side, weight):
        high, low = split_parts(weight)
        weight_ref[side * 3 * rows : side * 3 * rows + rows, :] = high
        weight_ref[side * 3 * rows + rows : side * 3 * rows + 2 * rows, :] = low
        weight_ref[side * 3 * rows + 2 * rows : side * 3 * rows + 3 * rows, :] = high

    def add_sums(side, left, right, left_again, right_low):
        both = dot_nt(left, right)
        total = both[:PART] + both[256 : 256 + PART]
        if left_again is not None:
            total = total + dot_nt(left_again, right_low)
        sums_ref[side] += total

    @pl.loop(0, edges // chunk)
    def _(c):
        at = pl.ds(pl.multiple_of(c * chunk, chunk), chunk)
        group = c // (edges // groups // chunk)
        slots = c * chunk + lax.broadcasted_iota(jnp.int32, (1, chunk), 1)
        alive = slots < live_ref[0]
        heads = jnp.where(alive, heads_ref[:, at], -1)
        tails = jnp.where(alive, tails_ref[:, at], -1)
        row = lax.broadcasted_iota(jnp.int32, (rows, chunk), 0)
        head_hot = one_hot(row == heads)
        tail_is = row == tails
        tail_hot = one_hot(tail_is)
        h = dot(cols_ref[0], head_hot)
        h = h[:PART] + h[PART:]
        t = dot(cols_ref[1], tail_hot)
        t = t[:PART] + t[PART:]
        r = rels_ref[:, at]
        h_re, h_im, t_re, t_im, r_re, r_im = h[:HALF], h[HALF:], t[:HALF], t[HALF:], r[:HALF], r[HALF:]
        put_query(0, jnp.concatenate([r_re * t_re + r_im * t_im, r_re * t_im - r_im * t_re], axis=0))
        put_query(1, jnp.concatenate([h_re * r_re - h_im * r_im, h_re * r_im + h_im * r_re], axis=0))
        grads = []
        for side in range(2):
            scores = dot(flip_ref[side], query_ref[side])
            chance = 0.5 * jnp.tanh(0.5 * scores) + 0.5
            count = counts_ref[group, 1 - side][:, :1]
            if side == 0:
                weight = chance * count
            else:
                hot = jnp.where(tail_is, 1.0, 0.0)
                weight = chance * (count + hot) - hot
            put_weight(side, weight)
            base = side * 3 * rows
            grads.append(dot(wide_ref[side], weight_ref[base : base + 3 * rows, :]))
            add_sums(
                side, query_ref[side, : 256 + PART, :], weight_ref[base : base + rows, :],
                query_ref[side, :PART, :], weight_ref[base + rows : base + 2 * rows, :],
            )
        qh_re, qh_im, qt_re, qt_im = grads[0][:HALF], grads[0][HALF:], grads[1][:HALF], grads[1][HALF:]
        dh = jnp.concatenate([qt_re * r_re + qt_im * r_im, qt_im * r_re - qt_re * r_im], axis=0)
        dt = jnp.concatenate([qh_re * r_re - qh_im * r_im, qh_re * r_im + qh_im * r_re], axis=0)
        dr = jnp.concatenate(
            [
                qt_re * h_re + qt_im * h_im + qh_re * t_re + qh_im * t_im,
                qt_im * h_re - qt_re * h_im + qh_re * t_im - qh_im * t_re,
            ],
            axis=0,
        )
        high, low = split_parts(dr)
        rel_grad_ref[:PART, at] = high
        rel_grad_ref[PART:, at] = low
        put_query(0, dh)
        add_sums(0, query_ref[0, : 256 + PART, :], head_hot, None, None)
        put_query(1, dt)
        add_sums(1, query_ref[1, : 256 + PART, :], tail_hot, None, None)

    for side, ref in enumerate((head_grad_ref, tail_grad_ref)):
        ref[:half, :] = sums_ref[side, :half, :]
        ref[half:, :] = sums_ref[side, HALF : HALF + half, :]


def edge_gradients(live, heads, tails, negs, head_blk, tail_blk, rels):
    width, rows = head_blk.shape
    edges = heads.shape[1]
    chunk = 512
    vmem = pl.BlockSpec(memory_space=pltpu.VMEM)
    return pl.pallas_call(
        edge_kernel,
        out_shape=(
            jax.ShapeDtypeStruct((width, rows), jnp.float32),
            jax.ShapeDtypeStruct((width, rows), jnp.float32),
            jax.ShapeDtypeStruct((2 * PART, edges), jnp.bfloat16),
        ),
        in_specs=[pl.BlockSpec(memory_space=pltpu.SMEM)] + [vmem] * 6,
        out_specs=(vmem, vmem, vmem),
        scratch_shapes=[
            pltpu.VMEM((2, 2 * PART, rows), jnp.bfloat16),
            pltpu.VMEM((2, rows, 768), jnp.bfloat16),
            pltpu.VMEM((2, PART, 3 * rows), jnp.bfloat16),
            pltpu.VMEM((2, 768, chunk), jnp.bfloat16),
            pltpu.VMEM((6 * rows, chunk), jnp.bfloat16),
            pltpu.VMEM((negs.shape[0], 2, rows, 128), jnp.float32),
            pltpu.VMEM((2, PART, rows), jnp.float32),
        ],
        compiler_params=pltpu.CompilerParams(vmem_limit_bytes=VMEM_LIMIT),
        cost_estimate=pl.CostEstimate(
            flops=40 * PART * rows * edges, bytes_accessed=4 * PART * edges, transcendentals=2 * rows * edges
        ),
        name="edge_gradients",
    )(live, heads, tails, negs, head_blk, tail_blk, rels)


def scatter_kernel(first_ref, ids_ref, grad_ref, out_ref, spread_ref):
    tiles, width, tile = out_ref.shape
    edges = ids_ref.shape[0]
    half = width // 2
    spread_ref[...] = jnp.broadcast_to(ids_ref[...], spread_ref.shape)

    @pl.loop(0, tiles // 2)
    def _(j):
        lane = lax.broadcasted_iota(jnp.int32, (edges, tile), 1)
        start = (first_ref[0] + 2 * j) * tile
        hot = jnp.concatenate(
            [one_hot(lane + start == spread_ref[...]), one_hot(lane + (start + tile) == spread_ref[...])], axis=1
        )
        cols = dot(grad_ref[...], hot)
        cols = cols[:PART] + cols[PART:]
        for side in range(2):
            part = cols[:, side * tile : (side + 1) * tile]
            out_ref[2 * j + side, :half, :] = part[:half]
            out_ref[2 * j + side, half:, :] = part[HALF : HALF + half]


def scatter_relations(first_tile, ids, grads, tiles, width):
    edges = grads.shape[1]
    vmem = pl.BlockSpec(memory_space=pltpu.VMEM)
    return pl.pallas_call(
        scatter_kernel,
        out_shape=jax.ShapeDtypeStruct((tiles, width, TILE), jnp.float32),
        in_specs=[pl.BlockSpec(memory_space=pltpu.SMEM), vmem, vmem],
        out_specs=vmem,
        scratch_shapes=[pltpu.VMEM((edges, TILE), jnp.int32)],
        compiler_params=pltpu.CompilerParams(vmem_limit_bytes=VMEM_LIMIT),
        cost_estimate=pl.CostEstimate(
            flops=4 * PART * edges * tiles * TILE, bytes_accessed=tiles * width * TILE * 4, transcendentals=0
        ),
        name="scatter_relations",
    )(first_tile, ids, grads)


def on_device(
    entities,
    entity_state,
    relations,
    relation_state,
    head_rows,
    relation_ids,
    tail_rows,
    neg_rows,
    edge_counts,
    matching,
):
    me = lax.axis_index("dom")
    core = me & 1
    xor_value = jnp.bitwise_xor(matching[0], me)
    width, count = relations.shape
    edges = head_rows.shape[1]
    mid = edges // 2
    half = -(-count // (64 * TILE)) * 32

    def gather(first):
        ids = relation_ids[:, first : first + mid]
        return lambda live, ids, table: gather_relations(live, ids, table, first), ids

    work, ids = gather(0)
    tail_blk, rels_low = partner_exchange(entities, xor_value, 0, 4, work, edge_counts, ids, relations)
    work, ids = gather(mid)
    tail_blk, rels_high = partner_exchange(tail_blk, xor_value, 4, 4, work, edge_counts, ids, relations)
    rels = jnp.concatenate([rels_low, rels_high], axis=1)
    head_grad, tail_grad, rel_grad = edge_gradients(
        edge_counts, head_rows, tail_rows, neg_rows[0], entities, tail_blk, rels
    )

    column = relation_ids.reshape(edges, 1)
    first_keep = (core * half).reshape(1)
    first_send = ((1 - core) * half).reshape(1)

    def scatter(first, ids, grads):
        return scatter_relations(first, ids, grads, half, width)

    def scatter_and_swap(first, ids, grads, send):
        received = xor_permute(send, 1)
        return scatter(first, ids, grads), received

    tail_grad, send = partner_exchange(tail_grad, xor_value, 0, 4, scatter, first_send, column, rel_grad)
    tail_grad, (keep, received) = partner_exchange(
        tail_grad, xor_value, 4, 4, scatter_and_swap, first_keep, column, rel_grad, send
    )
    combined = head_grad + tail_grad
    new_entity_state = entity_state + jnp.mean(combined * combined, axis=0)
    new_entities = entities - STEP_RATE * combined / jnp.sqrt(new_entity_state + EPSILON)[None, :]
    new_relations, new_relation_state = update_relations(keep, received, relations, relation_state)
    return (new_entities, new_entity_state, new_relations, new_relation_state)


def solution(mesh):
    in_specs = (
        P(None, "dom"),
        P("dom"),
        P(),
        P(),
        P("dom", None),
        P("dom", None),
        P("dom", None),
        P("dom", None, None, None),
        P("dom"),
        P("dom"),
    )
    out_specs = (P(None, "dom"), P("dom"), P(), P())
    return jax.shard_map(
        on_device, mesh=mesh, in_specs=in_specs, out_specs=out_specs, check_vma=False
    )
```

profile of v0, /device:TPU:1, one launch (start us, length us, event | category | flops | bytes accessed | tf_op | source)
XLA Modules:
  0.0 284.2 jit_solution(503118627502210926)
XLA Ops:
  2.6 46.3 %conditional.4 = (f32[200,384]{1,0:T(8,128)}, f32[208,1024]{1,0:T(8,128)S(1)}) conditional(s32[]{:T(128)} %clamp.9, (s32[1]{0:T(128)}, s32[1,1024]{1,0:T(1,128)S(1)}, f32[200,7424]{1,0:T(8,128)}, f32[200,384]{1,0:T(8,128)}) %tuple.264, (f32[200,384]{1,0:T(8,128)}, s32[1]{0:T(128)}, s32[1,1024]{1,0:T(1,128)S(1)}, ...), branch_computations={%region_0.0_spmd, %region_1.0_spmd, %region_2.0_spmd, %region_3.0_... | conditional | flops 6325010432 | bytes 7168056 | solution.py:36
  19.9 6.9 %collective-permute-start.11 = (f32[200,384]{1,0:T(8,128)}, f32[200,384]{1,0:T(8,128)}, u32[]{:S(2)}, u32[]{:S(2)}) collective-permute-start(f32[200,384]{1,0:T(8,128)} %get-tuple-element.592), channel_id=1, source_target_pairs={{0,12},{1,13},{2,14},{3,15},{4,8},{5,9},{6,10},{7,11},{8,4},{9,5},... | collective-permute-start | bytes 921608 | tf_op jit(solution)/shard_map/cond/branch_12_fun/ppermute | solution.py:25
  26.8 11.5 %gather_relations.44 = f32[208,1024]{1,0:T(8,128)S(1)} custom-call(s32[1]{0:T(128)} %get-tuple-element.593.live_ref, s32[1,1024]{1,0:T(1,128)S(1)} %get-tuple-element.594.ids_ref, f32[200,7424]{1,0:T(8,128)} %get-tuple-element.595.table_ref), custom_call_target="tpu_custom_call" | custom-call | flops 6325010432 | bytes 5939200 | tf_op jit(solution)/shard_map/cond/branch_12_fun/gather_relations/pallas_call | solution.py:147
  49.0 40.3 %conditional.5 = (f32[200,384]{1,0:T(8,128)}, f32[208,1024]{1,0:T(8,128)S(1)}) conditional(s32[]{:T(128)} %clamp.8, (s32[1]{0:T(128)}, s32[1,1024]{1,0:T(1,128)S(1)}, f32[200,7424]{1,0:T(8,128)}, f32[200,384]{1,0:T(8,128)}) %tuple.266, (f32[200,384]{1,0:T(8,128)}, s32[1]{0:T(128)}, s32[1,1024]{1,0:T(1,128)S(1)}, ...), branch_computations={%region_16.0_spmd, %region_17.0_spmd, %region_18.0_spmd, %region_1... | conditional | flops 6325010432 | bytes 7782456 | solution.py:36
  54.6 2.3 collective-permute-start.19
  56.9 11.5 %gather_relations.53 = f32[208,1024]{1,0:T(8,128)S(1)} custom-call(s32[1]{0:T(128)} %get-tuple-element.629.live_ref, s32[1,1024]{1,0:T(1,128)S(1)} %get-tuple-element.630.ids_ref, f32[200,7424]{1,0:T(8,128)} %get-tuple-element.631.table_ref), custom_call_target="tpu_custom_call" | custom-call | flops 6325010432 | bytes 5939200 | tf_op jit(solution)/shard_map/cond/branch_5_fun/gather_relations/pallas_call | solution.py:147
  90.3 18.0 %edge_gradients.1 = (f32[200,384]{1,0:T(8,128)S(1)}, f32[200,384]{1,0:T(8,128)S(1)}, bf16[416,2048]{1,0:T(8,128)(2,1)}) custom-call(s32[1]{0:T(128)S(6)} %copy.297.live_ref, s32[1,2048]{1,0:T(1,128)S(1)} %copy-done, s32[1,2048]{1,0:T(1,128)S(1)} %copy-done.1, s32[2,2,384]{2,1,0:T(2,128)S(1)} %bitcast.32, f32[200,384]{1,0:T(8,128)S(1)} %copy-done.4, ...), custom_call_target="tpu_custom_call" | custom-call | flops 6543114240 | bytes 1703936 | tf_op jit(solution)/shard_map/edge_gradients/pallas_call | solution.py:287
  108.3 27.8 %conditional.6 = (f32[200,384]{1,0:T(8,128)S(1)}, f32[32,200,128]{2,1,0:T(8,128)}) conditional(s32[]{:T(128)} %clamp.9, (s32[1]{0:T(128)}, s32[2048,1]{0,1:T(1,128)S(1)}, bf16[416,2048]{1,0:T(8,128)(2,1)}, f32[200,384]{1,0:T(8,128)S(1)}) %tuple.484, (f32[200,384]{1,0:T(8,128)S(1)}, s32[1]{0:T(128)}, ...), branch_computations={%region_32.0_spmd, %region_33.0_spmd, %region_34.0_spmd, %region_3... | conditional | flops 6979321856 | bytes 5136440 | solution.py:36
  117.9 4.4 %collective-permute-start.41 = (f32[200,384]{1,0:T(8,128)S(1)}, f32[200,384]{1,0:T(8,128)S(1)}, u32[]{:S(2)}, u32[]{:S(2)}) collective-permute-start(f32[200,384]{1,0:T(8,128)S(1)} %get-tuple-element.720), channel_id=1, source_target_pairs={{0,12},{1,13},{2,14},{3,15},{4,8},{5,9},{6,10},{7,11},{8,4},{9,5},... | collective-permute-start | bytes 921608 | tf_op jit(solution)/shard_map/cond/branch_12_fun/ppermute | solution.py:25
  122.6 13.4 %scatter_relations.44 = f32[32,200,128]{2,1,0:T(8,128)} custom-call(s32[1]{0:T(128)} %get-tuple-element.721.first_ref, s32[2048,1]{1,0:T(8,128)S(1)} %copy.126.ids_ref, bf16[416,2048]{1,0:T(8,128)(2,1)} %get-tuple-element.723.grad_ref), custom_call_target="tpu_custom_call" | custom-call | flops 6979321856 | bytes 3276800 | tf_op jit(solution)/shard_map/cond/branch_12_fun/scatter_relations/pallas_call | solution.py:337
  136.0 23.6 %conditional.7 = (f32[200,384]{1,0:T(8,128)S(1)}, f32[32,200,128]{2,1,0:T(8,128)S(1)}, f32[32,200,128]{2,1,0:T(8,128)}) conditional(s32[]{:T(128)} %clamp.8, (s32[1]{0:T(128)}, s32[2048,1]{0,1:T(1,128)S(1)}, bf16[416,2048]{1,0:T(8,128)(2,1)}, f32[32,200,128]{2,1,0:T(8,128)}, f32[200,384]{1,0:T(8,128)S(1)}) %tuple.485, ...), branch_computations={%region_48.0_spmd, %region_49.0_spmd, %region_50.0_spmd, %region_5... | conditional | flops 6979321856 | bytes 18243688 | solution.py:36
  144.2 11.6 %scatter_relations.53 = f32[32,200,128]{2,1,0:T(8,128)S(1)} custom-call(s32[1]{0:T(128)} %get-tuple-element.762.first_ref, s32[2048,1]{1,0:T(8,128)S(1)} %copy.135.ids_ref, bf16[416,2048]{1,0:T(8,128)(2,1)} %get-tuple-element.764.grad_ref), custom_call_target="tpu_custom_call" | custom-call | flops 6979321856 | bytes 3276800 | tf_op jit(solution)/shard_map/cond/branch_5_fun/scatter_relations/pallas_call | solution.py:337
  159.7 2.5 add.43
  162.2 26.1 %all_to_all.30 = f32[32,200,128]{2,1,0:T(8,128)} all-to-all(f32[32,200,128]{2,1,0:T(8,128)S(1)} %add.43), channel_id=1, replica_groups={{0,64,128,192},{2,66,130,194},{4,68,132,196},{6,70,134,198},{8,72,136,2..., dimensions={0} | all-to-all | bytes 6553600 | tf_op jit(solution)/shard_map/all_to_all | solution.py:51
  188.3 2.2 reduce_sum.53
  190.5 12.3 %all_to_all.31 = f32[8,200,128]{2,1,0:T(8,128)S(1)} all-to-all(f32[8,200,128]{2,1,0:T(8,128)S(1)} %reduce_sum.53), channel_id=1, replica_groups={{0,16,32,48},{2,18,34,50},{4,20,36,52},{6,22,38,54},{8,24,40,56},{10,26..., dimensions={0} | all-to-all | bytes 1638400 | tf_op jit(solution)/shard_map/all_to_all | solution.py:51
  202.9 11.8 %all_to_all.32 = f32[56,8,128]{2,1,0:T(8,128)S(1)} all-to-all(f32[56,8,128]{2,1,0:T(8,128)S(1)} %pad.4), channel_id=1, replica_groups={{0,2,4,6,8,10,12,14},{1,3,5,7,9,11,13,15},{16,18,20,22,24,26,28,30},{17..., dimensions={0} | all-to-all | bytes 458752 | tf_op jit(solution)/shard_map/all_to_all | solution.py:51
  215.4 3.4 %all-to-all-start.3 = ((f32[56,8,128]{2,1,0:T(8,128)}), f32[56,8,128]{2,1,0:T(8,128)S(1)}, u32[]{:S(2)}, u32[]{:S(2)}) async-start(f32[56,8,128]{2,1,0:T(8,128)} %bitcast.9), calls=%async_computation.3 | async-start | bytes 458752 | tf_op jit(solution)/shard_map/all_to_all | solution.py:51
  218.9 9.0 %all-to-all-done.3 = f32[56,8,128]{2,1,0:T(8,128)S(1)} async-done(((f32[56,8,128]{2,1,0:T(8,128)}), f32[56,8,128]{2,1,0:T(8,128)S(1)}, u32[]{:S(2)}, u32[]{:S(2)}) %all-to-all-start.3) | async-done | bytes 229408 | tf_op jit(solution)/shard_map/all_to_all | solution.py:51
  229.9 11.1 %all_to_all.33 = f32[8,208,128]{2,1,0:T(8,128)S(1)} all-to-all(f32[8,208,128]{2,1,0:T(8,128)S(1)} %bitcast.67), channel_id=1, replica_groups={{0,16,32,48},{2,18,34,50},{4,20,36,52},{6,22,38,54},{8,24,40,56},{10,26..., dimensions={0} | all-to-all | bytes 1703936 | tf_op jit(solution)/shard_map/all_to_all | solution.py:51
  241.3 25.2 %all_to_all.34 = f32[32,208,128]{2,1,0:T(8,128)S(1)} all-to-all(f32[32,208,128]{2,1,0:T(8,128)S(1)} %bitcast.33), channel_id=1, replica_groups={{0,64,128,192},{2,66,130,194},{4,68,132,196},{6,70,134,198},{8,72,136,2..., dimensions={0} | all-to-all | bytes 6815744 | tf_op jit(solution)/shard_map/all_to_all | solution.py:51
  266.5 7.4 %collective-permute-start.76 = (f32[32,208,128]{2,1,0:T(8,128)S(1)}, f32[32,208,128]{2,1,0:T(8,128)S(1)}, u32[]{:S(2)}, u32[]{:S(2)}) collective-permute-start(f32[32,208,128]{2,1,0:T(8,128)S(1)} %all_to_all.34), channel_id=1, source_target_pairs={{0,1},{1,0},{2,3},{3,2},{4,5},{5,4},{6,7},{7,6},{8,9},{9,8},{10,11... | collective-permute-start | bytes 10223624 | tf_op jit(solution)/shard_map/ppermute | solution.py:25
  275.3 4.2 %collective-permute-done.76 = f32[32,208,128]{2,1,0:T(8,128)S(1)} collective-permute-done((f32[32,208,128]{2,1,0:T(8,128)S(1)}, f32[32,208,128]{2,1,0:T(8,128)S(1)}, u32[]{:S(2)}, u32[]{:S(2)}) %collective-permute-start.76) | collective-permute-done | bytes 3407904 | tf_op jit(solution)/shard_map/ppermute | solution.py:25
  280.9 3.1 %copy_bitcast_fusion = f32[200,7424]{1,0:T(8,128)} fusion(f32[32,208,128]{2,1,0:T(8,128)S(1)} %broadcast_select_fusion, f32[26,208,128]{2,1,0:T(8,128)S(1)} %slice_select_fusion), kind=kLoop, calls=%fused_computation.4 | loop fusion | flops 1484800 | bytes 12115968 | tf_op jit(solution)/shard_map/reshape | solution.py:100
  (49 shorter events, 12.7 us)
Async XLA Ops:
  19.9 20.4 %collective-permute-start.11 = (f32[200,384]{1,0:T(8,128)}, f32[200,384]{1,0:T(8,128)}, u32[]{:S(2)}, u32[]{:S(2)}) collective-permute-start(f32[200,384]{1,0:T(8,128)} %get-tuple-element.592), channel_id=1, source_target_pairs={{0,12},{1,13},{2,14},{3,15},{4,8},{5,9},{6,10},{7,11},{8,4},{9,5},... | collective-permute-start | bytes 921608 | tf_op jit(solution)/shard_map/cond/branch_12_fun/ppermute | solution.py:25
  54.6 13.8 %collective-permute-start.19 = (f32[200,384]{1,0:T(8,128)}, f32[200,384]{1,0:T(8,128)S(1)}, u32[]{:S(2)}, u32[]{:S(2)}) collective-permute-start(f32[200,384]{1,0:T(8,128)} %get-tuple-element.628), channel_id=1, source_target_pairs={{0,80},{1,81},{2,82},{3,83},{4,84},{5,85},{6,86},{7,87},{8,88},{9,... | collective-permute-start | bytes 921608 | tf_op jit(solution)/shard_map/cond/branch_5_fun/ppermute | solution.py:25
  89.3 0.7 copy-start
  89.3 0.7 copy-start.1
  89.3 0.7 copy-start.2
  89.3 1.0 copy-start.4
  90.3 18.0 %copy-start.3 = (s32[1,2048]{1,0:T(1,128)S(1)}, s32[1,2048]{1,0:T(1,128)}, u32[]{:S(2)}) copy-start(s32[1,2048]{1,0:T(1,128)} %param.79) | copy-start | bytes 24580
  117.9 18.1 %collective-permute-start.41 = (f32[200,384]{1,0:T(8,128)S(1)}, f32[200,384]{1,0:T(8,128)S(1)}, u32[]{:S(2)}, u32[]{:S(2)}) collective-permute-start(f32[200,384]{1,0:T(8,128)S(1)} %get-tuple-element.720), channel_id=1, source_target_pairs={{0,12},{1,13},{2,14},{3,15},{4,8},{5,9},{6,10},{7,11},{8,4},{9,5},... | collective-permute-start | bytes 921608 | tf_op jit(solution)/shard_map/cond/branch_12_fun/ppermute | solution.py:25
  142.0 13.8 %collective-permute-start.55 = (f32[32,200,128]{2,1,0:T(8,128)}, f32[32,200,128]{2,1,0:T(8,128)}, u32[]{:S(2)}, u32[]{:S(2)}) collective-permute-start(f32[32,200,128]{2,1,0:T(8,128)} %get-tuple-element.765), channel_id=1, source_target_pairs={{0,1},{1,0},{2,3},{3,2},{4,5},{5,4},{6,7},{7,6},{8,9},{9,8},{10,11... | collective-permute-start | bytes 9830408 | tf_op jit(solution)/shard_map/cond/branch_5_fun/ppermute | solution.py:25
  143.6 12.2 %collective-permute-start.54 = (f32[200,384]{1,0:T(8,128)S(1)}, f32[200,384]{1,0:T(8,128)S(1)}, u32[]{:S(2)}, u32[]{:S(2)}) collective-permute-start(f32[200,384]{1,0:T(8,128)S(1)} %get-tuple-element.761), channel_id=1, source_target_pairs={{0,80},{1,81},{2,82},{3,83},{4,84},{5,85},{6,86},{7,87},{8,88},{9,... | collective-permute-start | bytes 921608 | tf_op jit(solution)/shard_map/cond/branch_5_fun/ppermute | solution.py:25
  215.4 12.4 %all-to-all-start.3 = ((f32[56,8,128]{2,1,0:T(8,128)}), f32[56,8,128]{2,1,0:T(8,128)S(1)}, u32[]{:S(2)}, u32[]{:S(2)}) async-start(f32[56,8,128]{2,1,0:T(8,128)} %bitcast.9), calls=%async_computation.3 | async-start | bytes 458752 | tf_op jit(solution)/shard_map/all_to_all | solution.py:51
  241.3 32.7 %copy-start.6 = (f32[384]{0:T(512)S(1)}, f32[384]{0:T(512)}, u32[]{:S(2)}) copy-start(f32[384]{0:T(512)} %param.75) | copy-start | bytes 4612
  241.3 33.2 %copy-start.5 = (f32[200,384]{1,0:T(8,128)S(1)}, f32[200,384]{1,0:T(8,128)}, u32[]{:S(2)}) copy-start(f32[200,384]{1,0:T(8,128)} %head_ref.1) | copy-start | bytes 921604
  266.5 13.1 %collective-permute-start.76 = (f32[32,208,128]{2,1,0:T(8,128)S(1)}, f32[32,208,128]{2,1,0:T(8,128)S(1)}, u32[]{:S(2)}, u32[]{:S(2)}) collective-permute-start(f32[32,208,128]{2,1,0:T(8,128)S(1)} %all_to_all.34), channel_id=1, source_target_pairs={{0,1},{1,0},{2,3},{3,2},{4,5},{5,4},{6,7},{7,6},{8,9},{9,8},{10,11... | collective-permute-start | bytes 10223624 | tf_op jit(solution)/shard_map/ppermute | solution.py:25
where the time goes:
time: 288 us; the launch traced here: 284 us
  blocking collectives  86.5 us (30%)
  loops' own time  71.2 us (25%)
  Pallas kernels  66 us (23%)
  starting transfers between devices  26.2 us (9%)
  waiting for transfers between devices  15.1 us (5%)
  other arithmetic  12.7 us (4%)
  local copies, waits for them, and re-layouts  4.24 us (1%)
    all_to_all x5, blocking collectives, swap_chunks(): lax.all_to_all(value, 'dom', 0, 0, axis_index_groups=groups, tiled=True)  86.5 us
    another operation x4, loops' own time, partner_exchange(): return lax.switch(pick, branches, value, *operands)  71.2 us
    pallas_call x2, Pallas kernels, scatter_relations(): pl.pallas_call(scatter_kernel, out_shape=jax.ShapeDtypeStruct((tiles, wid...  25 us
    pallas_call x2, Pallas kernels, gather_relations(): pl.pallas_call(functools.partial(gather_kernel, first_slot), out_shape=ja...  23 us
    ppermute x6, starting transfers between devices, xor_permute(): return lax.ppermute(value, 'dom', [(i, i ^ mask) for i in range(size)])  22.8 us
    pallas_call x1, Pallas kernels, edge_gradients(): pl.pallas_call(edge_kernel, out_shape=(jax.ShapeDtypeStruct((width, rows)...  18 us
    all_to_all x1, waiting for transfers between devices, swap_chunks(): lax.all_to_all(value, 'dom', 0, 0, axis_index_groups=groups, tiled=True)  8.98 us
    ppermute x6, waiting for transfers between devices, xor_permute(): return lax.ppermute(value, 'dom', [(i, i ^ mask) for i in range(size)])  6.15 us
  transfers between devices with their start and end apart: 7, of which 3 were waited for; matrix products, arithmetic and copies ran while one was open for 1% of the time, Pallas kernels for 17%

commit v1 on v0

--- a/solution.py
+++ b/solution.py
@@ -119,41 +119,78 @@
     return jnp.where(condition, 1.0, 0.0).astype(jnp.bfloat16)
 
 
-def gather_kernel(first_slot, live_ref, ids_ref, table_ref, out_ref, parts):
+def gather_kernel(first_slot, live_ref, ids_ref, table_ref, out_ref, table, parts, sums, ready):
     width, count = table_ref.shape
-    high, low = split_parts(table_ref[...])
-    blank = jnp.zeros((PART - width, count), jnp.bfloat16)
-    parts[:PART, :] = jnp.concatenate([high, blank], axis=0)
-    parts[PART:, :] = jnp.concatenate([low, blank], axis=0)
     edges = ids_ref.shape[1]
-    chunk = 256
     half = width // 2
-
-    @pl.loop(0, edges // chunk)
+    depth = 7
+    step = depth * 256
+    pieces = count // step
+
+    def piece(i, size=step):
+        at = pl.ds(pl.multiple_of(i * step, 256), size)
+        return pltpu.make_async_copy(table_ref.at[:, at], table.at[:, at], ready.at[i])
+
+    rest = count - pieces * step
+    for i in range(pieces):
+        piece(i).start()
+    if rest:
+        piece(pieces, rest).start()
+    sums[...] = jnp.zeros_like(sums)
+
+    def add_tiles(i, tiles):
+        @pl.loop(0, tiles)
+        def _(k):
+            at = pl.ds(pl.multiple_of(i * step + k * 256, 256), 256)
+            tile = jnp.concatenate([table[:, at], jnp.zeros((PART - width, 256), jnp.float32)], axis=0)
+            there = pl.ds(pl.multiple_of(k * 256, 256), 256)
+            high, low = split_parts(tile)
+            parts[:PART, there] = high
+            parts[PART:, there] = low
+
+        @pl.loop(0, edges // 256)
+        def _(c):
+            there = pl.ds(pl.multiple_of(c * 256, 256), 256)
+            slots = first_slot + c * 256 + lax.broadcasted_iota(jnp.int32, (1, 256), 1)
+            ids = jnp.where(slots < live_ref[0], ids_ref[:, there], -1) - i * step
+            row = lax.broadcasted_iota(jnp.int32, (256, 256), 0)
+            cols = sums[:, there]
+            for k in range(tiles):
+                cols += dot(parts[:, k * 256 : (k + 1) * 256], one_hot(row + k * 256 == ids))
+            sums[:, there] = cols
+
+    @pl.loop(0, pieces)
+    def _(i):
+        piece(i).wait()
+        add_tiles(i, depth)
+
+    if rest:
+        piece(pieces, rest).wait()
+        add_tiles(pieces, rest // 256)
+
+    @pl.loop(0, edges // 256)
     def _(c):
-        at = pl.ds(pl.multiple_of(c * chunk, chunk), chunk)
-        slots = first_slot + c * chunk + lax.broadcasted_iota(jnp.int32, (1, chunk), 1)
-        ids = jnp.where(slots < live_ref[0], ids_ref[:, at], -1)
-        hot = one_hot(lax.broadcasted_iota(jnp.int32, (count, chunk), 0) == ids)
-        cols = dot(parts[...], hot)
-        cols = cols[:PART] + cols[PART:]
-        out_ref[:HALF, at] = cols[:HALF]
-        out_ref[HALF:, at] = cols[half : half + HALF]
+        there = pl.ds(pl.multiple_of(c * 256, 256), 256)
+        cols = sums[:PART, there] + sums[PART:, there]
+        out_ref[:HALF, there] = cols[:HALF]
+        out_ref[HALF:, there] = cols[half : half + HALF]
 
 
 def gather_relations(live, ids, relations, first_slot):
     width, count = relations.shape
     edges = ids.shape[1]
+    vmem = pl.BlockSpec(memory_space=pltpu.VMEM)
     return pl.pallas_call(
         functools.partial(gather_kernel, first_slot),
         out_shape=jax.ShapeDtypeStruct((PART, edges), jnp.float32),
-        in_specs=[
-            pl.BlockSpec(memory_space=pltpu.SMEM),
-            pl.BlockSpec(memory_space=pltpu.VMEM),
-            pl.BlockSpec(memory_space=pltpu.VMEM),
+        in_specs=[pl.BlockSpec(memory_space=pltpu.SMEM), vmem, pl.BlockSpec(memory_space=pl.ANY)],
+        out_specs=vmem,
+        scratch_shapes=[
+            pltpu.VMEM((width, count), jnp.float32),
+            pltpu.VMEM((2 * PART, 7 * 256), jnp.bfloat16),
+            pltpu.VMEM((2 * PART, edges), jnp.float32),
+            pltpu.SemaphoreType.DMA((8,)),
         ],
-        out_specs=pl.BlockSpec(memory_space=pltpu.VMEM),
-        scratch_shapes=[pltpu.VMEM((2 * PART, count), jnp.bfloat16)],
         compiler_params=pltpu.CompilerParams(vmem_limit_bytes=VMEM_LIMIT),
         cost_estimate=pl.CostEstimate(
             flops=4 * PART * count * edges, bytes_accessed=width * count * 4, transcendentals=0
@@ -318,12 +355,14 @@
 
     @pl.loop(0, tiles // 2)
     def _(j):
-        lane = lax.broadcasted_iota(jnp.int32, (edges, tile), 1)
         start = (first_ref[0] + 2 * j) * tile
-        hot = jnp.concatenate(
-            [one_hot(lane + start == spread_ref[...]), one_hot(lane + (start + tile) == spread_ref[...])], axis=1
-        )
-        cols = dot(grad_ref[...], hot)
+        lane = lax.broadcasted_iota(jnp.int32, (256, tile), 1)
+        cols = None
+        for c in range(0, edges, 256):
+            ids = spread_ref[c : c + 256, :]
+            hot = jnp.concatenate([one_hot(lane + start == ids), one_hot(lane + (start + tile) == ids)], axis=1)
+            part = dot(grad_ref[:, c : c + 256], hot)
+            cols = part if cols is None else cols + part
         cols = cols[:PART] + cols[PART:]
         for side in range(2):
             part = cols[:, side * tile : (side + 1) * tile]

time: 288 us -> 257 us (0.89)
  loops' own time: 71.2 us -> 32.3 us
  starting transfers between devices: 26.2 us -> 31.1 us
  Pallas kernels: 66 us -> 69.3 us
    another operation x4, loops' own time: 71.2 us -> 32.3 us  [partner_exchange(): return lax.switch(pick, branches, value, *operands)]
    ppermute x6, starting transfers between devices: 22.8 us -> 27.7 us  [xor_permute(): return lax.ppermute(value, 'dom', [(i, i ^ mask) for i in range(size)])]
    pallas_call x2, Pallas kernels: 23 us -> 26.3 us  [gather_relations(): pl.pallas_call(functools.partial(gather_kernel, first_slot), out_shape=ja...]
  transfers between devices with their start and end apart: 7 -> 7, of which waited for: 3 -> 4; matrix products, arithmetic and copies ran while one was open for 1% -> 1% of each run, Pallas kernels for 17% -> 20%
where the time goes in v1:
time: 257 us; the launch traced here: 254 us
  blocking collectives  88.5 us (34%)
  Pallas kernels  69.3 us (27%)
  loops' own time  32.3 us (13%)
  starting transfers between devices  31.1 us (12%)
  waiting for transfers between devices  13.7 us (5%)
  other arithmetic  12.7 us (5%)
  local copies, waits for them, and re-layouts  4.24 us (2%)
    all_to_all x5, blocking collectives, swap_chunks(): lax.all_to_all(value, 'dom', 0, 0, axis_index_groups=groups, tiled=True)  88.5 us
    another operation x4, loops' own time, partner_exchange(): return lax.switch(pick, branches, value, *operands)  32.3 us
    ppermute x6, starting transfers between devices, xor_permute(): return lax.ppermute(value, 'dom', [(i, i ^ mask) for i in range(size)])  27.7 us
    pallas_call x2, Pallas kernels, gather_relations(): pl.pallas_call(functools.partial(gather_kernel, first_slot), out_shape=ja...  26.3 us
    pallas_call x2, Pallas kernels, scatter_relations(): pl.pallas_call(scatter_kernel, out_shape=jax.ShapeDtypeStruct((tiles, wid...  25 us
    pallas_call x1, Pallas kernels, edge_gradients(): pl.pallas_call(edge_kernel, out_shape=(jax.ShapeDtypeStruct((width, rows)...  18 us
    all_to_all x1, waiting for transfers between devices, swap_chunks(): lax.all_to_all(value, 'dom', 0, 0, axis_index_groups=groups, tiled=True)  8.98 us
  transfers between devices with their start and end apart: 7, of which 4 were waited for; matrix products, arithmetic and copies ran while one was open for 1% of the time, Pallas kernels for 20%

profile of v1, /device:TPU:1, one launch (start us, length us, event | category | flops | bytes accessed | tf_op | source)
XLA Modules:
  0.0 254.2 jit_solution(1276843055681341828)
XLA Ops:
  2.6 34.8 %conditional.4 = (f32[200,384]{1,0:T(8,128)}, f32[208,1024]{1,0:T(8,128)S(1)}) conditional(s32[]{:T(128)} %clamp.9, (s32[1]{0:T(128)}, s32[1,1024]{1,0:T(1,128)S(1)}, f32[200,7424]{1,0:T(8,128)}, f32[200,384]{1,0:T(8,128)}) %tuple.264, (f32[200,384]{1,0:T(8,128)}, s32[1]{0:T(128)}, s32[1,1024]{1,0:T(1,128)S(1)}, ...), branch_computations={%region_0.0_spmd, %region_1.0_spmd, %region_2.0_spmd, %region_3.0_... | conditional | flops 6325010432 | bytes 7168056 | solution.py:36
  2.7 7.8 %collective-permute-start.7 = (f32[200,384]{1,0:T(8,128)}, f32[200,384]{1,0:T(8,128)}, u32[]{:S(2)}, u32[]{:S(2)}) collective-permute-start(f32[200,384]{1,0:T(8,128)} %get-tuple-element.576), channel_id=1, source_target_pairs={{0,8},{1,9},{2,10},{3,11},{4,12},{5,13},{6,14},{7,15},{8,0},{9,1},... | collective-permute-start | bytes 921608 | tf_op jit(solution)/shard_map/cond/branch_8_fun/ppermute | solution.py:25
  10.5 13.2 %gather_relations.40 = f32[208,1024]{1,0:T(8,128)S(1)} custom-call(s32[1]{0:T(128)} %get-tuple-element.577.live_ref, s32[1,1024]{1,0:T(1,128)S(1)} %get-tuple-element.578.ids_ref, f32[200,7424]{1,0:T(8,128)} %get-tuple-element.579.table_ref), custom_call_target="tpu_custom_call" | custom-call | flops 6325010432 | bytes 5939200 | tf_op jit(solution)/shard_map/cond/branch_8_fun/gather_relations/pallas_call | solution.py:183
  37.5 26.5 %conditional.5 = (f32[200,384]{1,0:T(8,128)}, f32[208,1024]{1,0:T(8,128)S(1)}) conditional(s32[]{:T(128)} %clamp.8, (s32[1]{0:T(128)}, s32[1,1024]{1,0:T(1,128)S(1)}, f32[200,7424]{1,0:T(8,128)}, f32[200,384]{1,0:T(8,128)}) %tuple.266, (f32[200,384]{1,0:T(8,128)}, s32[1]{0:T(128)}, s32[1,1024]{1,0:T(1,128)S(1)}, ...), branch_computations={%region_16.0_spmd, %region_17.0_spmd, %region_18.0_spmd, %region_1... | conditional | flops 6325010432 | bytes 7782456 | solution.py:36
  44.7 5.2 %collective-permute-start.28 = (f32[200,384]{1,0:T(8,128)}, f32[200,384]{1,0:T(8,128)S(1)}, u32[]{:S(2)}, u32[]{:S(2)}) collective-permute-start(f32[200,384]{1,0:T(8,128)} %get-tuple-element.664), channel_id=1, source_target_pairs={{0,224},{1,225},{2,226},{3,227},{4,228},{5,229},{6,230},{7,231},{8... | collective-permute-start | bytes 921608 | tf_op jit(solution)/shard_map/cond/branch_14_fun/ppermute | solution.py:25
  49.9 13.2 %gather_relations.62 = f32[208,1024]{1,0:T(8,128)S(1)} custom-call(s32[1]{0:T(128)} %get-tuple-element.665.live_ref, s32[1,1024]{1,0:T(1,128)S(1)} %get-tuple-element.666.ids_ref, f32[200,7424]{1,0:T(8,128)} %get-tuple-element.667.table_ref), custom_call_target="tpu_custom_call" | custom-call | flops 6325010432 | bytes 5939200 | tf_op jit(solution)/shard_map/cond/branch_14_fun/gather_relations/pallas_call | solution.py:183
  65.0 18.0 %edge_gradients.1 = (f32[200,384]{1,0:T(8,128)S(1)}, f32[200,384]{1,0:T(8,128)S(1)}, bf16[416,2048]{1,0:T(8,128)(2,1)}) custom-call(s32[1]{0:T(128)S(6)} %copy.297.live_ref, s32[1,2048]{1,0:T(1,128)S(1)} %copy-done, s32[1,2048]{1,0:T(1,128)S(1)} %copy-done.1, s32[2,2,384]{2,1,0:T(2,128)S(1)} %bitcast.32, f32[200,384]{1,0:T(8,128)S(1)} %copy-done.4, ...), custom_call_target="tpu_custom_call" | custom-call | flops 6543114240 | bytes 1703936 | tf_op jit(solution)/shard_map/edge_gradients/pallas_call | solution.py:324
  83.0 14.3 %conditional.6 = (f32[200,384]{1,0:T(8,128)S(1)}, f32[32,200,128]{2,1,0:T(8,128)}) conditional(s32[]{:T(128)} %clamp.9, (s32[1]{0:T(128)}, s32[2048,1]{0,1:T(1,128)S(1)}, bf16[416,2048]{1,0:T(8,128)(2,1)}, f32[200,384]{1,0:T(8,128)S(1)}) %tuple.484, (f32[200,384]{1,0:T(8,128)S(1)}, s32[1]{0:T(128)}, ...), branch_computations={%region_32.0_spmd, %region_33.0_spmd, %region_34.0_spmd, %region_3... | conditional | flops 6979321856 | bytes 5136440 | solution.py:36
  83.8 13.4 %scatter_relations.40 = f32[32,200,128]{2,1,0:T(8,128)} custom-call(s32[1]{0:T(128)} %get-tuple-element.705.first_ref, s32[2048,1]{1,0:T(8,128)S(1)} %copy.122.ids_ref, bf16[416,2048]{1,0:T(8,128)(2,1)} %get-tuple-element.707.grad_ref), custom_call_target="tpu_custom_call" | custom-call | flops 6979321856 | bytes 3276800 | tf_op jit(solution)/shard_map/cond/branch_8_fun/scatter_relations/pallas_call | solution.py:376
  97.3 30.3 %conditional.7 = (f32[200,384]{1,0:T(8,128)S(1)}, f32[32,200,128]{2,1,0:T(8,128)S(1)}, f32[32,200,128]{2,1,0:T(8,128)}) conditional(s32[]{:T(128)} %clamp.8, (s32[1]{0:T(128)}, s32[2048,1]{0,1:T(1,128)S(1)}, bf16[416,2048]{1,0:T(8,128)(2,1)}, f32[32,200,128]{2,1,0:T(8,128)}, f32[200,384]{1,0:T(8,128)S(1)}) %tuple.485, ...), branch_computations={%region_48.0_spmd, %region_49.0_spmd, %region_50.0_spmd, %region_5... | conditional | flops 6979321856 | bytes 18243688 | solution.py:36
  107.9 7.0 %collective-permute-start.73 = (f32[32,200,128]{2,1,0:T(8,128)}, f32[32,200,128]{2,1,0:T(8,128)}, u32[]{:S(2)}, u32[]{:S(2)}) collective-permute-start(f32[32,200,128]{2,1,0:T(8,128)} %get-tuple-element.810), channel_id=1, source_target_pairs={{0,1},{1,0},{2,3},{3,2},{4,5},{5,4},{6,7},{7,6},{8,9},{9,8},{10,11... | collective-permute-start | bytes 9830408 | tf_op jit(solution)/shard_map/cond/branch_14_fun/ppermute | solution.py:25
  115.3 11.6 %scatter_relations.62 = f32[32,200,128]{2,1,0:T(8,128)S(1)} custom-call(s32[1]{0:T(128)} %get-tuple-element.807.first_ref, s32[2048,1]{1,0:T(8,128)S(1)} %copy.144.ids_ref, bf16[416,2048]{1,0:T(8,128)(2,1)} %get-tuple-element.809.grad_ref), custom_call_target="tpu_custom_call" | custom-call | flops 6979321856 | bytes 3276800 | tf_op jit(solution)/shard_map/cond/branch_14_fun/scatter_relations/pallas_call | solution.py:376
  127.6 2.5 add.43
  130.1 25.6 %all_to_all.30 = f32[32,200,128]{2,1,0:T(8,128)} all-to-all(f32[32,200,128]{2,1,0:T(8,128)S(1)} %add.43), channel_id=1, replica_groups={{0,64,128,192},{2,66,130,194},{4,68,132,196},{6,70,134,198},{8,72,136,2..., dimensions={0} | all-to-all | bytes 6553600 | tf_op jit(solution)/shard_map/all_to_all | solution.py:51
  155.8 2.2 reduce_sum.53
  158.0 12.1 %all_to_all.31 = f32[8,200,128]{2,1,0:T(8,128)S(1)} all-to-all(f32[8,200,128]{2,1,0:T(8,128)S(1)} %reduce_sum.53), channel_id=1, replica_groups={{0,16,32,48},{2,18,34,50},{4,20,36,52},{6,22,38,54},{8,24,40,56},{10,26..., dimensions={0} | all-to-all | bytes 1638400 | tf_op jit(solution)/shard_map/all_to_all | solution.py:51
  170.1 14.5 %all_to_all.32 = f32[56,8,128]{2,1,0:T(8,128)S(1)} all-to-all(f32[56,8,128]{2,1,0:T(8,128)S(1)} %pad.4), channel_id=1, replica_groups={{0,2,4,6,8,10,12,14},{1,3,5,7,9,11,13,15},{16,18,20,22,24,26,28,30},{17..., dimensions={0} | all-to-all | bytes 458752 | tf_op jit(solution)/shard_map/all_to_all | solution.py:51
  185.4 3.4 %all-to-all-start.3 = ((f32[56,8,128]{2,1,0:T(8,128)}), f32[56,8,128]{2,1,0:T(8,128)S(1)}, u32[]{:S(2)}, u32[]{:S(2)}) async-start(f32[56,8,128]{2,1,0:T(8,128)} %bitcast.9), calls=%async_computation.3 | async-start | bytes 458752 | tf_op jit(solution)/shard_map/all_to_all | solution.py:51
  188.8 9.0 %all-to-all-done.3 = f32[56,8,128]{2,1,0:T(8,128)S(1)} async-done(((f32[56,8,128]{2,1,0:T(8,128)}), f32[56,8,128]{2,1,0:T(8,128)S(1)}, u32[]{:S(2)}, u32[]{:S(2)}) %all-to-all-start.3) | async-done | bytes 229408 | tf_op jit(solution)/shard_map/all_to_all | solution.py:51
  199.9 11.1 %all_to_all.33 = f32[8,208,128]{2,1,0:T(8,128)S(1)} all-to-all(f32[8,208,128]{2,1,0:T(8,128)S(1)} %bitcast.67), channel_id=1, replica_groups={{0,16,32,48},{2,18,34,50},{4,20,36,52},{6,22,38,54},{8,24,40,56},{10,26..., dimensions={0} | all-to-all | bytes 1703936 | tf_op jit(solution)/shard_map/all_to_all | solution.py:51
  211.2 25.2 %all_to_all.34 = f32[32,208,128]{2,1,0:T(8,128)S(1)} all-to-all(f32[32,208,128]{2,1,0:T(8,128)S(1)} %bitcast.33), channel_id=1, replica_groups={{0,64,128,192},{2,66,130,194},{4,68,132,196},{6,70,134,198},{8,72,136,2..., dimensions={0} | all-to-all | bytes 6815744 | tf_op jit(solution)/shard_map/all_to_all | solution.py:51
  236.4 7.4 %collective-permute-start.76 = (f32[32,208,128]{2,1,0:T(8,128)S(1)}, f32[32,208,128]{2,1,0:T(8,128)S(1)}, u32[]{:S(2)}, u32[]{:S(2)}) collective-permute-start(f32[32,208,128]{2,1,0:T(8,128)S(1)} %all_to_all.34), channel_id=1, source_target_pairs={{0,1},{1,0},{2,3},{3,2},{4,5},{5,4},{6,7},{7,6},{8,9},{9,8},{10,11... | collective-permute-start | bytes 10223624 | tf_op jit(solution)/shard_map/ppermute | solution.py:25
  245.3 4.2 %collective-permute-done.76 = f32[32,208,128]{2,1,0:T(8,128)S(1)} collective-permute-done((f32[32,208,128]{2,1,0:T(8,128)S(1)}, f32[32,208,128]{2,1,0:T(8,128)S(1)}, u32[]{:S(2)}, u32[]{:S(2)}) %collective-permute-start.76) | collective-permute-done | bytes 3407904 | tf_op jit(solution)/shard_map/ppermute | solution.py:25
  250.8 3.1 %copy_bitcast_fusion = f32[200,7424]{1,0:T(8,128)} fusion(f32[32,208,128]{2,1,0:T(8,128)S(1)} %broadcast_select_fusion, f32[26,208,128]{2,1,0:T(8,128)S(1)} %slice_select_fusion), kind=kLoop, calls=%fused_computation.4 | loop fusion | flops 1484800 | bytes 12115968 | tf_op jit(solution)/shard_map/reshape | solution.py:100
  (49 shorter events, 9.8 us)
Async XLA Ops:
  2.7 21.0 %collective-permute-start.7 = (f32[200,384]{1,0:T(8,128)}, f32[200,384]{1,0:T(8,128)}, u32[]{:S(2)}, u32[]{:S(2)}) collective-permute-start(f32[200,384]{1,0:T(8,128)} %get-tuple-element.576), channel_id=1, source_target_pairs={{0,8},{1,9},{2,10},{3,11},{4,12},{5,13},{6,14},{7,15},{8,0},{9,1},... | collective-permute-start | bytes 921608 | tf_op jit(solution)/shard_map/cond/branch_8_fun/ppermute | solution.py:25
  44.7 18.4 %collective-permute-start.28 = (f32[200,384]{1,0:T(8,128)}, f32[200,384]{1,0:T(8,128)S(1)}, u32[]{:S(2)}, u32[]{:S(2)}) collective-permute-start(f32[200,384]{1,0:T(8,128)} %get-tuple-element.664), channel_id=1, source_target_pairs={{0,224},{1,225},{2,226},{3,227},{4,228},{5,229},{6,230},{7,231},{8... | collective-permute-start | bytes 921608 | tf_op jit(solution)/shard_map/cond/branch_14_fun/ppermute | solution.py:25
  64.0 0.7 copy-start
  64.0 0.7 copy-start.1
  64.0 0.7 copy-start.2
  64.0 1.0 copy-start.4
  65.0 18.0 %copy-start.3 = (s32[1,2048]{1,0:T(1,128)S(1)}, s32[1,2048]{1,0:T(1,128)}, u32[]{:S(2)}) copy-start(s32[1,2048]{1,0:T(1,128)} %param.79) | copy-start | bytes 24580
  83.2 14.1 %collective-permute-start.37 = (f32[200,384]{1,0:T(8,128)S(1)}, f32[200,384]{1,0:T(8,128)S(1)}, u32[]{:S(2)}, u32[]{:S(2)}) collective-permute-start(f32[200,384]{1,0:T(8,128)S(1)} %get-tuple-element.704), channel_id=1, source_target_pairs={{0,8},{1,9},{2,10},{3,11},{4,12},{5,13},{6,14},{7,15},{8,0},{9,1},... | collective-permute-start | bytes 921608 | tf_op jit(solution)/shard_map/cond/branch_8_fun/ppermute | solution.py:25
  107.9 19.5 %collective-permute-start.73 = (f32[32,200,128]{2,1,0:T(8,128)}, f32[32,200,128]{2,1,0:T(8,128)}, u32[]{:S(2)}, u32[]{:S(2)}) collective-permute-start(f32[32,200,128]{2,1,0:T(8,128)} %get-tuple-element.810), channel_id=1, source_target_pairs={{0,1},{1,0},{2,3},{3,2},{4,5},{5,4},{6,7},{7,6},{8,9},{9,8},{10,11... | collective-permute-start | bytes 9830408 | tf_op jit(solution)/shard_map/cond/branch_14_fun/ppermute | solution.py:25
  114.9 12.5 %collective-permute-start.72 = (f32[200,384]{1,0:T(8,128)S(1)}, f32[200,384]{1,0:T(8,128)S(1)}, u32[]{:S(2)}, u32[]{:S(2)}) collective-permute-start(f32[200,384]{1,0:T(8,128)S(1)} %get-tuple-element.806), channel_id=1, source_target_pairs={{0,224},{1,225},{2,226},{3,227},{4,228},{5,229},{6,230},{7,231},{8... | collective-permute-start | bytes 921608 | tf_op jit(solution)/shard_map/cond/branch_14_fun/ppermute | solution.py:25
  185.4 12.4 %all-to-all-start.3 = ((f32[56,8,128]{2,1,0:T(8,128)}), f32[56,8,128]{2,1,0:T(8,128)S(1)}, u32[]{:S(2)}, u32[]{:S(2)}) async-start(f32[56,8,128]{2,1,0:T(8,128)} %bitcast.9), calls=%async_computation.3 | async-start | bytes 458752 | tf_op jit(solution)/shard_map/all_to_all | solution.py:51
  211.2 32.7 %copy-start.6 = (f32[384]{0:T(512)S(1)}, f32[384]{0:T(512)}, u32[]{:S(2)}) copy-start(f32[384]{0:T(512)} %param.75) | copy-start | bytes 4612
  211.2 33.2 %copy-start.5 = (f32[200,384]{1,0:T(8,128)S(1)}, f32[200,384]{1,0:T(8,128)}, u32[]{:S(2)}) copy-start(f32[200,384]{1,0:T(8,128)} %head_ref.1) | copy-start | bytes 921604
  236.4 13.1 %collective-permute-start.76 = (f32[32,208,128]{2,1,0:T(8,128)S(1)}, f32[32,208,128]{2,1,0:T(8,128)S(1)}, u32[]{:S(2)}, u32[]{:S(2)}) collective-permute-start(f32[32,208,128]{2,1,0:T(8,128)S(1)} %all_to_all.34), channel_id=1, source_target_pairs={{0,1},{1,0},{2,3},{3,2},{4,5},{5,4},{6,7},{7,6},{8,9},{9,8},{10,11... | collective-permute-start | bytes 10223624 | tf_op jit(solution)/shard_map/ppermute | solution.py:25

commit v2 on v1

--- a/solution.py
+++ b/solution.py
@@ -14,15 +14,22 @@
 STEP_RATE = 0.3
 EPSILON = 1e-08
 
-CORE = (0, 1)
-Z = (1, 3)
-Y = (4, 2)
-X = (6, 2)
+
+def pair_permute(value, low_mask, high_mask):
+    size = lax.axis_size("dom")
+    return lax.ppermute(value, "dom", [(i, i ^ (high_mask if i & 1 else low_mask)) for i in range(size)])
 
 
 def xor_permute(value, mask):
-    size = lax.axis_size("dom")
-    return lax.ppermute(value, "dom", [(i, i ^ mask) for i in range(size)])
+    return pair_permute(value, mask, mask)
+
+
+def outer_permute(value, k):
+    return pair_permute(value, k << 6, k << 4)
+
+
+def inner_permute(value, k):
+    return pair_permute(value, k << 4, k << 6)
 
 
 def partner_exchange(value, xor_value, low, width, work, *operands):
@@ -36,69 +43,46 @@
     return lax.switch(pick, branches, value, *operands)
 
 
-def members(axis, cores):
-    low, width = axis
-    mask = (2**width - 1) << low
+def z_groups():
     size = lax.axis_size("dom")
-    return [
-        [base | (k << low) for k in range(2**width)]
-        for base in range(size)
-        if base & mask == 0 and (base & 1) in cores
-    ]
-
-
-def swap_chunks(value, groups):
-    return lax.all_to_all(value, "dom", 0, 0, axis_index_groups=groups, tiled=True)
-
-
-def scatter_sum(value, groups):
-    ways = len(groups[0])
-    moved = swap_chunks(value, groups)
-    return jnp.sum(moved.reshape((ways, value.shape[0] // ways) + value.shape[1:]), axis=0)
-
-
-def spread(value, groups):
-    ways = len(groups[0])
-    copies = jnp.broadcast_to(value[None], (ways,) + value.shape)
-    return swap_chunks(copies.reshape((ways * value.shape[0],) + value.shape[1:]), groups)
-
-
-def update_relations(keep, received, relations, relation_state):
-    me = lax.axis_index("dom")
-    core, cy, cx = me & 1, (me >> 4) & 3, (me >> 6) & 3
+    return [[base | (k << 1) for k in range(8)] for base in range(size) if base & 14 == 0]
+
+
+def z_swap(value):
+    return lax.all_to_all(value, "dom", 0, 0, axis_index_groups=z_groups(), tiled=True)
+
+
+def z_total(part):
+    rows = part.shape[0]
+    flat = jnp.pad(part, ((0, -rows % 8), (0, 0), (0, 0)))
+    share = flat.shape[0] // 8
+    mine = jnp.sum(z_swap(flat).reshape(8, share, 8, TILE), axis=0)
+    return z_swap(jnp.tile(mine, (8, 1, 1)))[:rows]
+
+
+def update_relations(place, keep, received, relations, relation_state):
     half, width, _ = keep.shape
-    first = members(X, (0,)) + members(Y, (1,))
-    second = members(Y, (0,)) + members(X, (1,))
-    along_z = members(Z, (0, 1))
-
-    part = keep + received
-    part = scatter_sum(part, first)
-    part = scatter_sum(part, second)
-    owned = part.shape[0]
-    flat = part.reshape(owned * width // 8, 8, TILE)
-    rows = flat.shape[0]
-    flat = jnp.pad(flat, ((0, -rows % 8), (0, 0), (0, 0)))
-    flat = spread(scatter_sum(flat, along_z), along_z)
-    total = flat[:rows].reshape(owned, width, TILE).transpose(1, 0, 2).reshape(width, owned * TILE)
-
-    outer = jnp.where(core == 0, cx, cy)
-    inner = jnp.where(core == 0, cy, cx)
-    start = (core * half + outer * (half // 4) + inner * owned) * TILE
+    chunk, owned = half // 4, half // 16
+    parts = [keep[k * chunk : (k + 1) * chunk] + received[k * chunk : (k + 1) * chunk] for k in range(4)]
+    moved = [outer_permute(parts[k], k) for k in (1, 2, 3)]
+    part = parts[0] + moved[0] + moved[1] + moved[2]
+    moved = [inner_permute(part[k * owned : (k + 1) * owned], k) for k in (1, 2, 3)]
+    part = part[:owned] + moved[0] + moved[1] + moved[2]
+    total = z_total(part.reshape(owned * width // 8, 8, TILE))
+    total = total.reshape(owned, width, TILE).transpose(1, 0, 2).reshape(width, owned * TILE)
+
+    start = tile_at(0, place, place[0]) * TILE
     values = lax.dynamic_slice_in_dim(relations, start, owned * TILE, 1)
     state = lax.dynamic_slice_in_dim(relation_state, start, owned * TILE)
     new_state = state + jnp.mean(total * total, axis=0)
     new_values = values - STEP_RATE * total / jnp.sqrt(new_state + EPSILON)[None, :]
     packed = jnp.concatenate([new_values, jnp.broadcast_to(new_state[None], (8, owned * TILE))], axis=0)
     packed = packed.reshape(width + 8, owned, TILE).transpose(1, 0, 2)
-    packed = spread(packed, second)
-    packed = spread(packed, first)
-    other = xor_permute(packed, 1)
-    low = jnp.where(core == 0, packed, other)
-    high = jnp.where(core == 0, other, packed)
-    count = relations.shape[1]
-    both = jnp.concatenate([low, high[: count // TILE - half]], axis=0)
-    new_relations = both[:, :width].transpose(1, 0, 2).reshape(width, count)
-    return new_relations, both[:, width].reshape(count)
+    packed = jnp.concatenate([packed] + [inner_permute(packed, k) for k in (1, 2, 3)], axis=0)
+    mine = [packed] + [outer_permute(packed, k) for k in (1, 2, 3)]
+    others = [xor_permute(value, 1) for value in mine]
+    new_relations, state_rows = place_columns(place, mine, others, width, relations.shape[1])
+    return new_relations, state_rows[0]
 
 
 def split_parts(x):
@@ -347,15 +331,22 @@
     )(live, heads, tails, negs, head_blk, tail_blk, rels)
 
 
-def scatter_kernel(first_ref, ids_ref, grad_ref, out_ref, spread_ref):
+def tile_at(position, place_ref, core):
+    outer = (position // 8) ^ place_ref[1 + core]
+    inner = (position // 2 % 4) ^ place_ref[2 - core]
+    return core * 32 + outer * 8 + inner * 2 + position % 2
+
+
+def scatter_kernel(other, place_ref, ids_ref, grad_ref, out_ref, spread_ref):
     tiles, width, tile = out_ref.shape
+    core = jnp.where(other, 1 - place_ref[0], place_ref[0])
     edges = ids_ref.shape[0]
     half = width // 2
     spread_ref[...] = jnp.broadcast_to(ids_ref[...], spread_ref.shape)
 
     @pl.loop(0, tiles // 2)
     def _(j):
-        start = (first_ref[0] + 2 * j) * tile
+        start = tile_at(2 * j, place_ref, core) * tile
         lane = lax.broadcasted_iota(jnp.int32, (256, tile), 1)
         cols = None
         for c in range(0, edges, 256):
@@ -370,11 +361,11 @@
             out_ref[2 * j + side, half:, :] = part[HALF : HALF + half]
 
 
-def scatter_relations(first_tile, ids, grads, tiles, width):
+def scatter_relations(other, place, ids, grads, tiles, width):
     edges = grads.shape[1]
     vmem = pl.BlockSpec(memory_space=pltpu.VMEM)
     return pl.pallas_call(
-        scatter_kernel,
+        functools.partial(scatter_kernel, other),
         out_shape=jax.ShapeDtypeStruct((tiles, width, TILE), jnp.float32),
         in_specs=[pl.BlockSpec(memory_space=pltpu.SMEM), vmem, vmem],
         out_specs=vmem,
@@ -384,7 +375,45 @@
             flops=4 * PART * edges * tiles * TILE, bytes_accessed=tiles * width * TILE * 4, transcendentals=0
         ),
         name="scatter_relations",
-    )(first_tile, ids, grads)
+    )(place, ids, grads)
+
+
+def place_kernel(place_ref, *refs):
+    chunks, (cols_ref, state_ref, done) = refs[:8], refs[8:]
+    width, count = cols_ref.shape
+    for core in range(2):
+        for chunk in range(4):
+            source = chunks[core * 4 + chunk]
+            whose = jnp.where(core == 0, place_ref[0], 1 - place_ref[0])
+
+            @pl.loop(0, 8)
+            def _(j):
+                tile = tile_at(chunk * 8 + j, place_ref, whose)
+
+                @pl.when(tile < count // TILE)
+                def _():
+                    at = pl.ds(pl.multiple_of(tile * TILE, TILE), TILE)
+                    pltpu.make_async_copy(source.at[j, :width, :], cols_ref.at[:, at], done.at[0]).start()
+                    pltpu.make_async_copy(source.at[j, width:, :], state_ref.at[:, at], done.at[1]).start()
+
+    pltpu.make_async_copy(cols_ref, cols_ref, done.at[0]).wait()
+    pltpu.make_async_copy(state_ref, state_ref, done.at[1]).wait()
+
+
+def place_columns(place, mine, others, width, count):
+    hbm = pl.BlockSpec(memory_space=pl.ANY)
+    return pl.pallas_call(
+        place_kernel,
+        out_shape=(
+            jax.ShapeDtypeStruct((width, count), jnp.float32),
+            jax.ShapeDtypeStruct((8, count), jnp.float32),
+        ),
+        in_specs=[pl.BlockSpec(memory_space=pltpu.SMEM)] + [hbm] * 8,
+        out_specs=(hbm, hbm),
+        scratch_shapes=[pltpu.SemaphoreType.DMA((2,))],
+        cost_estimate=pl.CostEstimate(flops=0, bytes_accessed=8 * width * count, transcendentals=0),
+        name="place_columns",
+    )(place, *mine, *others)
 
 
 def on_device(
@@ -421,24 +450,23 @@
     )
 
     column = relation_ids.reshape(edges, 1)
-    first_keep = (core * half).reshape(1)
-    first_send = ((1 - core) * half).reshape(1)
-
-    def scatter(first, ids, grads):
-        return scatter_relations(first, ids, grads, half, width)
-
-    def scatter_and_swap(first, ids, grads, send):
+    place = jnp.stack([core, (me >> 6) & 3, (me >> 4) & 3])
+
+    def scatter(place, ids, grads):
+        return scatter_relations(True, place, ids, grads, half, width)
+
+    def scatter_and_swap(place, ids, grads, send):
         received = xor_permute(send, 1)
-        return scatter(first, ids, grads), received
-
-    tail_grad, send = partner_exchange(tail_grad, xor_value, 0, 4, scatter, first_send, column, rel_grad)
+        return scatter_relations(False, place, ids, grads, half, width), received
+
+    tail_grad, send = partner_exchange(tail_grad, xor_value, 0, 4, scatter, place, column, rel_grad)
     tail_grad, (keep, received) = partner_exchange(
-        tail_grad, xor_value, 4, 4, scatter_and_swap, first_keep, column, rel_grad, send
+        tail_grad, xor_value, 4, 4, scatter_and_swap, place, column, rel_grad, send
     )
     combined = head_grad + tail_grad
     new_entity_state = entity_state + jnp.mean(combined * combined, axis=0)
     new_entities = entities - STEP_RATE * combined / jnp.sqrt(new_entity_state + EPSILON)[None, :]
-    new_relations, new_relation_state = update_relations(keep, received, relations, relation_state)
+    new_relations, new_relation_state = update_relations(place, keep, received, relations, relation_state)
     return (new_entities, new_entity_state, new_relations, new_relation_state)
 
 

time: 257 us -> 459 us (1.79); the launches traced: 254 us -> 451 us
  Pallas kernels: 69.3 us -> 258 us
  blocking collectives: 88.5 us -> 11.8 us
  starting transfers between devices: 31.1 us -> 79.8 us
  waiting for transfers between devices: 13.7 us -> 48.2 us
  other arithmetic: 12.7 us -> 6.91 us
    pallas_call x2 -> x3, Pallas kernels: 25 us -> 214 us  [the longest x1 189 us: place_columns(): pl.pallas_call(place_kernel, out_shape=(jax.ShapeDtypeStruct((width, coun...]
    all_to_all x5 -> x1, blocking collectives: 88.5 us -> 11.8 us  [z_swap(): lax.all_to_all(value, 'dom', 0, 0, axis_index_groups=z_groups(), tiled=True)]
    ppermute x6 -> x21, starting transfers between devices: 27.7 us -> 76.4 us  [pair_permute(): lax.ppermute(value, 'dom', [(i, i ^ (high_mask if i & 1 else low_mask)) f...]
    ppermute x6 -> x21, waiting for transfers between devices: 4.75 us -> 41.2 us  [pair_permute(): lax.ppermute(value, 'dom', [(i, i ^ (high_mask if i & 1 else low_mask)) f...]
  transfers between devices with their start and end apart: 7 -> 22, of which waited for: 4 -> 13; matrix products, arithmetic and copies ran while one was open for 1% -> 1% of each run, Pallas kernels for 20% -> 11%
where the time goes in v2:
time: 459 us; the launch traced here: 451 us
  Pallas kernels  258 us (56%)
  starting transfers between devices  79.8 us (17%)
  waiting for transfers between devices  48.2 us (11%)
  loops' own time  34 us (7%)
  blocking collectives  11.8 us (3%)
  local copies, waits for them, and re-layouts  8.15 us (2%)
  other arithmetic  6.91 us (2%)
    pallas_call x1, Pallas kernels, place_columns(): pl.pallas_call(place_kernel, out_shape=(jax.ShapeDtypeStruct((width, coun...  189 us
    ppermute x21, starting transfers between devices, pair_permute(): lax.ppermute(value, 'dom', [(i, i ^ (high_mask if i & 1 else low_mask)) f...  76.4 us
    ppermute x21, waiting for transfers between devices, pair_permute(): lax.ppermute(value, 'dom', [(i, i ^ (high_mask if i & 1 else low_mask)) f...  41.2 us
    another operation x4, loops' own time, partner_exchange(): return lax.switch(pick, branches, value, *operands)  34 us
    pallas_call x2, Pallas kernels, gather_relations(): pl.pallas_call(functools.partial(gather_kernel, first_slot), out_shape=ja...  26.3 us
    pallas_call x2, Pallas kernels, scatter_relations(): pl.pallas_call(functools.partial(scatter_kernel, other), out_shape=jax.Sh...  25.3 us
    pallas_call x1, Pallas kernels, edge_gradients(): pl.pallas_call(edge_kernel, out_shape=(jax.ShapeDtypeStruct((width, rows)...  17.9 us
    all_to_all x1, blocking collectives, z_swap(): lax.all_to_all(value, 'dom', 0, 0, axis_index_groups=z_groups(), tiled=True)  11.8 us
  transfers between devices with their start and end apart: 22, of which 13 were waited for; matrix products, arithmetic and copies ran while one was open for 1% of the time, Pallas kernels for 11%

profile of v2, /device:TPU:1, one launch (start us, length us, event | category | flops | bytes accessed | tf_op | source)
XLA Modules:
  0.0 451.1 jit_solution(5109960920798499892)
XLA Ops:
  2.6 26.4 %conditional.4 = (f32[200,384]{1,0:T(8,128)}, f32[208,1024]{1,0:T(8,128)S(1)}) conditional(s32[]{:T(128)} %clamp.9, (s32[1]{0:T(128)}, s32[1,1024]{1,0:T(1,128)S(1)}, f32[200,7424]{1,0:T(8,128)}, f32[200,384]{1,0:T(8,128)}) %tuple.264, (f32[200,384]{1,0:T(8,128)}, s32[1]{0:T(128)}, s32[1,1024]{1,0:T(1,128)S(1)}, ...), branch_computations={%region_0.0_spmd, %region_1.0_spmd, %region_2.0_spmd, %region_3.0_... | conditional | flops 6325010432 | bytes 7168056 | solution.py:43
  7.2 7.5 %collective-permute-start.12 = (f32[200,384]{1,0:T(8,128)}, f32[200,384]{1,0:T(8,128)}, u32[]{:S(2)}, u32[]{:S(2)}) collective-permute-start(f32[200,384]{1,0:T(8,128)} %get-tuple-element.596), channel_id=1, source_target_pairs={{0,13},{1,12},{2,15},{3,14},{4,9},{5,8},{6,11},{7,10},{8,5},{9,4},... | collective-permute-start | bytes 921608 | tf_op jit(solution)/shard_map/cond/branch_13_fun/ppermute | solution.py:20
  14.7 13.2 %gather_relations.45 = f32[208,1024]{1,0:T(8,128)S(1)} custom-call(s32[1]{0:T(128)} %get-tuple-element.597.live_ref, s32[1,1024]{1,0:T(1,128)S(1)} %get-tuple-element.598.ids_ref, f32[200,7424]{1,0:T(8,128)} %get-tuple-element.599.table_ref), custom_call_target="tpu_custom_call" | custom-call | flops 6325010432 | bytes 5939200 | tf_op jit(solution)/shard_map/cond/branch_13_fun/gather_relations/pallas_call | solution.py:167
  29.1 26.9 %conditional.5 = (f32[200,384]{1,0:T(8,128)}, f32[208,1024]{1,0:T(8,128)S(1)}) conditional(s32[]{:T(128)} %clamp.8, (s32[1]{0:T(128)}, s32[1,1024]{1,0:T(1,128)S(1)}, f32[200,7424]{1,0:T(8,128)}, f32[200,384]{1,0:T(8,128)}) %tuple.266, (f32[200,384]{1,0:T(8,128)}, s32[1]{0:T(128)}, s32[1,1024]{1,0:T(1,128)S(1)}, ...), branch_computations={%region_16.0_spmd, %region_17.0_spmd, %region_18.0_spmd, %region_1... | conditional | flops 6325010432 | bytes 7782456 | solution.py:43
  32.1 13.2 %gather_relations.50 = f32[208,1024]{1,0:T(8,128)S(1)} custom-call(s32[1]{0:T(128)} %get-tuple-element.617.live_ref, s32[1,1024]{1,0:T(1,128)S(1)} %get-tuple-element.618.ids_ref, f32[200,7424]{1,0:T(8,128)} %get-tuple-element.619.table_ref), custom_call_target="tpu_custom_call" | custom-call | flops 6325010432 | bytes 5939200 | tf_op jit(solution)/shard_map/cond/branch_2_fun/gather_relations/pallas_call | solution.py:167
  57.1 17.9 %edge_gradients.1 = (f32[200,384]{1,0:T(8,128)S(1)}, f32[200,384]{1,0:T(8,128)S(1)}, bf16[416,2048]{1,0:T(8,128)(2,1)}) custom-call(s32[1]{0:T(128)S(6)} %copy.229.live_ref, s32[1,2048]{1,0:T(1,128)S(1)} %copy-done, s32[1,2048]{1,0:T(1,128)S(1)} %copy-done.1, s32[2,2,384]{2,1,0:T(2,128)S(1)} %bitcast.30, f32[200,384]{1,0:T(8,128)S(1)} %copy-done.5, ...), custom_call_target="tpu_custom_call" | custom-call | flops 6543114240 | bytes 1703936 | tf_op jit(solution)/shard_map/edge_gradients/pallas_call | solution.py:308
  75.0 19.1 %conditional.6 = (f32[200,384]{1,0:T(8,128)S(1)}, f32[32,200,128]{2,1,0:T(8,128)}) conditional(s32[]{:T(128)} %clamp.9, (s32[3]{0:T(128)S(1)}, s32[2048,1]{0,1:T(1,128)S(1)}, bf16[416,2048]{1,0:T(8,128)(2,1)}, f32[200,384]{1,0:T(8,128)S(1)}) %tuple.425, (f32[200,384]{1,0:T(8,128)S(1)}, s32[3]{0:T(128)S(1)}, ...), branch_computations={%region_32.0_spmd, %region_33.0_spmd, %region_34.0_spmd, %region_3... | conditional | flops 6979321856 | bytes 5136440 | solution.py:43
  75.3 4.9 %collective-permute-start.42 = (f32[200,384]{1,0:T(8,128)S(1)}, f32[200,384]{1,0:T(8,128)S(1)}, u32[]{:S(2)}, u32[]{:S(2)}) collective-permute-start(f32[200,384]{1,0:T(8,128)S(1)} %get-tuple-element.724), channel_id=1, source_target_pairs={{0,13},{1,12},{2,15},{3,14},{4,9},{5,8},{6,11},{7,10},{8,5},{9,4},... | collective-permute-start | bytes 921608 | tf_op jit(solution)/shard_map/cond/branch_13_fun/ppermute | solution.py:20
  80.6 13.5 %scatter_relations.45 = f32[32,200,128]{2,1,0:T(8,128)} custom-call(s32[3]{0:T(128)S(1)} %get-tuple-element.725.place_ref, s32[2048,1]{1,0:T(8,128)S(1)} %copy.60.ids_ref, bf16[416,2048]{1,0:T(8,128)(2,1)} %get-tuple-element.727.grad_ref), custom_call_target="tpu_custom_call" | custom-call | flops 6979321856 | bytes 3276800 | tf_op jit(solution)/shard_map/cond/branch_13_fun/scatter_relations/pallas_call | solution.py:367
  94.1 31.1 %conditional.7 = (f32[200,384]{1,0:T(8,128)S(1)}, f32[32,200,128]{2,1,0:T(8,128)S(1)}, f32[32,200,128]{2,1,0:T(8,128)}) conditional(s32[]{:T(128)} %clamp.8, (s32[3]{0:T(128)S(1)}, s32[2048,1]{0,1:T(1,128)S(1)}, bf16[416,2048]{1,0:T(8,128)(2,1)}, f32[32,200,128]{2,1,0:T(8,128)}, f32[200,384]{1,0:T(8,128)S(1)}) %tuple.426, ...), branch_computations={%region_48.0_spmd, %region_49.0_spmd, %region_50.0_spmd, %region_5... | conditional | flops 6979321856 | bytes 18243688 | solution.py:43
  95.2 11.8 %scatter_relations.50 = f32[32,200,128]{2,1,0:T(8,128)S(1)} custom-call(s32[3]{0:T(128)S(1)} %get-tuple-element.747.place_ref, s32[2048,1]{1,0:T(8,128)S(1)} %copy.65.ids_ref, bf16[416,2048]{1,0:T(8,128)(2,1)} %get-tuple-element.749.grad_ref), custom_call_target="tpu_custom_call" | custom-call | flops 6979321856 | bytes 3276800 | tf_op jit(solution)/shard_map/cond/branch_2_fun/scatter_relations/pallas_call | solution.py:367
  131.1 7.6 %collective-permute-done.76 = f32[8,200,128]{2,1,0:T(8,128)S(1)} collective-permute-done((f32[8,200,128]{2,1,0:T(8,128)S(1)}, f32[8,200,128]{2,1,0:T(8,128)S(1)}, u32[]{:S(2)}, u32[]{:S(2)}) %collective-permute-start.76) | collective-permute-done | bytes 819232 | tf_op jit(solution)/shard_map/ppermute | solution.py:20
  138.7 9.8 %collective-permute-done.78 = f32[8,200,128]{2,1,0:T(8,128)S(1)} collective-permute-done((f32[8,200,128]{2,1,0:T(8,128)S(1)}, f32[8,200,128]{2,1,0:T(8,128)S(1)}, u32[]{:S(2)}, u32[]{:S(2)}) %collective-permute-start.78) | collective-permute-done | bytes 819232 | tf_op jit(solution)/shard_map/ppermute | solution.py:20
  156.0 3.1 collective-permute-done.81
  160.5 11.8 %all_to_all.10 = f32[56,8,128]{2,1,0:T(8,128)S(1)} all-to-all(f32[56,8,128]{2,1,0:T(8,128)S(1)} %pad.4), channel_id=1, replica_groups={{0,2,4,6,8,10,12,14},{1,3,5,7,9,11,13,15},{16,18,20,22,24,26,28,30},{17..., dimensions={0} | all-to-all | bytes 458752 | tf_op jit(solution)/shard_map/all_to_all | solution.py:52
  173.0 3.4 all-to-all-start.1
  178.3 7.0 %all-to-all-done.1 = f32[56,8,128]{2,1,0:T(8,128)S(1)} async-done(((f32[56,8,128]{2,1,0:T(8,128)}), f32[56,8,128]{2,1,0:T(8,128)S(1)}, u32[]{:S(2)}, u32[]{:S(2)}) %all-to-all-start.1) | async-done | bytes 229408 | tf_op jit(solution)/shard_map/all_to_all | solution.py:52
  190.6 3.8 collective-permute-done.84
  199.5 11.2 %collective-permute-start.88 = (f32[8,208,128]{2,1,0:T(8,128)S(1)}, f32[8,208,128]{2,1,0:T(8,128)S(1)}, u32[]{:S(2)}, u32[]{:S(2)}) collective-permute-start(f32[8,208,128]{2,1,0:T(8,128)S(1)} %pad_maximum_fusion.1.refs_0_), channel_id=1, source_target_pairs={{0,1},{1,0},{2,3},{3,2},{4,5},{5,4},{6,7},{7,6},{8,9},{9,8},{10,11... | collective-permute-start | bytes 2555912 | tf_op jit(solution)/shard_map/ppermute | solution.py:20
  210.7 10.1 %collective-permute-done.87.refs_3_ = f32[8,208,128]{2,1,0:T(8,128)S(1)} collective-permute-done((f32[8,208,128]{2,1,0:T(8,128)S(1)}, f32[8,208,128]{2,1,0:T(8,128)S(1)}, u32[]{:S(2)}, u32[]{:S(2)}) %collective-permute-start.87) | collective-permute-done | bytes 852000 | tf_op jit(solution)/shard_map/ppermute | solution.py:20
  220.8 11.7 %collective-permute-start.91 = (f32[8,208,128]{2,1,0:T(8,128)S(1)}, f32[8,208,128]{2,1,0:T(8,128)S(1)}, u32[]{:S(2)}, u32[]{:S(2)}) collective-permute-start(f32[8,208,128]{2,1,0:T(8,128)S(1)} %collective-permute-done.87.refs_3_), channel_id=1, source_target_pairs={{0,1},{1,0},{2,3},{3,2},{4,5},{5,4},{6,7},{7,6},{8,9},{9,8},{10,11... | collective-permute-start | bytes 2555912 | tf_op jit(solution)/shard_map/ppermute | solution.py:20
  232.5 11.8 %collective-permute-start.90 = (f32[8,208,128]{2,1,0:T(8,128)S(1)}, f32[8,208,128]{2,1,0:T(8,128)S(1)}, u32[]{:S(2)}, u32[]{:S(2)}) collective-permute-start(f32[8,208,128]{2,1,0:T(8,128)S(1)} %collective-permute-done.86.refs_2_), channel_id=1, source_target_pairs={{0,1},{1,0},{2,3},{3,2},{4,5},{5,4},{6,7},{7,6},{8,9},{9,8},{10,11... | collective-permute-start | bytes 2555912 | tf_op jit(solution)/shard_map/ppermute | solution.py:20
  244.3 11.8 %collective-permute-start.89 = (f32[8,208,128]{2,1,0:T(8,128)S(1)}, f32[8,208,128]{2,1,0:T(8,128)}, u32[]{:S(2)}, u32[]{:S(2)}) collective-permute-start(f32[8,208,128]{2,1,0:T(8,128)S(1)} %collective-permute-done.85.refs_1_), channel_id=1, source_target_pairs={{0,1},{1,0},{2,3},{3,2},{4,5},{5,4},{6,7},{7,6},{8,9},{9,8},{10,11... | collective-permute-start | bytes 2555912 | tf_op jit(solution)/shard_map/ppermute | solution.py:20
  260.2 188.8 %place_columns.1 = (f32[200,7424]{1,0:T(8,128)}, f32[8,7424]{1,0:T(8,128)}) custom-call(s32[3]{0:T(128)S(1)} %pad_add_fusion.place_ref, f32[8,208,128]{2,1,0:T(8,128)} %copy-done.4, f32[8,208,128]{2,1,0:T(8,128)} %copy-done.9, f32[8,208,128]{2,1,0:T(8,128)} %copy-done.8, f32[8,208,128]{2,1,0:T(8,128)} %copy-done.7, f32[8,208,128]{2,1,0:T(8,128)} %copy-done.10, ...), custom_call_target="tpu_custom_call" | custom-call | bytes 11878400 | tf_op jit(solution)/shard_map/place_columns/pallas_call | solution.py:405
  (87 shorter events, 39.4 us)
Async XLA Ops:
  7.2 21.5 %collective-permute-start.12 = (f32[200,384]{1,0:T(8,128)}, f32[200,384]{1,0:T(8,128)}, u32[]{:S(2)}, u32[]{:S(2)}) collective-permute-start(f32[200,384]{1,0:T(8,128)} %get-tuple-element.596), channel_id=1, source_target_pairs={{0,13},{1,12},{2,15},{3,14},{4,9},{5,8},{6,11},{7,10},{8,5},{9,4},... | collective-permute-start | bytes 921608 | tf_op jit(solution)/shard_map/cond/branch_13_fun/ppermute | solution.py:20
  29.1 16.2 %collective-permute-start.16 = (f32[200,384]{1,0:T(8,128)}, f32[200,384]{1,0:T(8,128)S(1)}, u32[]{:S(2)}, u32[]{:S(2)}) collective-permute-start(f32[200,384]{1,0:T(8,128)} %get-tuple-element.616), channel_id=1, source_target_pairs={{0,32},{1,33},{2,34},{3,35},{4,36},{5,37},{6,38},{7,39},{8,40},{9,... | collective-permute-start | bytes 921608 | tf_op jit(solution)/shard_map/cond/branch_2_fun/ppermute | solution.py:20
  75.3 18.8 %collective-permute-start.42 = (f32[200,384]{1,0:T(8,128)S(1)}, f32[200,384]{1,0:T(8,128)S(1)}, u32[]{:S(2)}, u32[]{:S(2)}) collective-permute-start(f32[200,384]{1,0:T(8,128)S(1)} %get-tuple-element.724), channel_id=1, source_target_pairs={{0,13},{1,12},{2,15},{3,14},{4,9},{5,8},{6,11},{7,10},{8,5},{9,4},... | collective-permute-start | bytes 921608 | tf_op jit(solution)/shard_map/cond/branch_13_fun/ppermute | solution.py:20
  94.6 12.5 %collective-permute-start.49 = (f32[32,200,128]{2,1,0:T(8,128)}, f32[32,200,128]{2,1,0:T(8,128)}, u32[]{:S(2)}, u32[]{:S(2)}) collective-permute-start(f32[32,200,128]{2,1,0:T(8,128)} %get-tuple-element.750), channel_id=1, source_target_pairs={{0,1},{1,0},{2,3},{3,2},{4,5},{5,4},{6,7},{7,6},{8,9},{9,8},{10,11... | collective-permute-start | bytes 9830408 | tf_op jit(solution)/shard_map/cond/branch_2_fun/ppermute | solution.py:20
  94.7 12.3 %collective-permute-start.48 = (f32[200,384]{1,0:T(8,128)S(1)}, f32[200,384]{1,0:T(8,128)S(1)}, u32[]{:S(2)}, u32[]{:S(2)}) collective-permute-start(f32[200,384]{1,0:T(8,128)S(1)} %get-tuple-element.746), channel_id=1, source_target_pairs={{0,32},{1,33},{2,34},{3,35},{4,36},{5,37},{6,38},{7,39},{8,40},{9,... | collective-permute-start | bytes 921608 | tf_op jit(solution)/shard_map/cond/branch_2_fun/ppermute | solution.py:20
  127.1 11.6 %collective-permute-start.76 = (f32[8,200,128]{2,1,0:T(8,128)S(1)}, f32[8,200,128]{2,1,0:T(8,128)S(1)}, u32[]{:S(2)}, u32[]{:S(2)}) collective-permute-start(f32[8,200,128]{2,1,0:T(8,128)S(1)} %get-tuple-element.1140), channel_id=1, source_target_pairs={{0,64},{1,17},{2,66},{3,19},{4,68},{5,21},{6,70},{7,23},{8,72},{9,... | collective-permute-start | bytes 2457608 | tf_op jit(solution)/shard_map/ppermute | solution.py:20
  128.5 19.9 %collective-permute-start.78 = (f32[8,200,128]{2,1,0:T(8,128)S(1)}, f32[8,200,128]{2,1,0:T(8,128)S(1)}, u32[]{:S(2)}, u32[]{:S(2)}) collective-permute-start(f32[8,200,128]{2,1,0:T(8,128)S(1)} %get-tuple-element.1141), channel_id=1, source_target_pairs={{0,192},{1,49},{2,194},{3,51},{4,196},{5,53},{6,198},{7,55},{8,200... | collective-permute-start | bytes 2457608 | tf_op jit(solution)/shard_map/ppermute | solution.py:20
  130.3 19.5 %collective-permute-start.77 = (f32[8,200,128]{2,1,0:T(8,128)S(1)}, f32[8,200,128]{2,1,0:T(8,128)S(1)}, u32[]{:S(2)}, u32[]{:S(2)}) collective-permute-start(f32[8,200,128]{2,1,0:T(8,128)S(1)} %get-tuple-element.1142), channel_id=1, source_target_pairs={{0,128},{1,33},{2,130},{3,35},{4,132},{5,37},{6,134},{7,39},{8,136... | collective-permute-start | bytes 2457608 | tf_op jit(solution)/shard_map/ppermute | solution.py:20
  151.3 4.7 %collective-permute-start.79 = (f32[2,200,128]{2,1,0:T(8,128)S(1)}, f32[2,200,128]{2,1,0:T(8,128)S(1)}, u32[]{:S(2)}, u32[]{:S(2)}) collective-permute-start(f32[2,200,128]{2,1,0:T(8,128)S(1)} %get-tuple-element.1143), channel_id=1, source_target_pairs={{0,16},{1,65},{2,18},{3,67},{4,20},{5,69},{6,22},{7,71},{8,24},{9,... | collective-permute-start | bytes 614408 | tf_op jit(solution)/shard_map/ppermute | solution.py:20
  152.4 6.7 %collective-permute-start.81 = (f32[2,200,128]{2,1,0:T(8,128)S(1)}, f32[2,200,128]{2,1,0:T(8,128)S(1)}, u32[]{:S(2)}, u32[]{:S(2)}) collective-permute-start(f32[2,200,128]{2,1,0:T(8,128)S(1)} %get-tuple-element.1144), channel_id=1, source_target_pairs={{0,48},{1,193},{2,50},{3,195},{4,52},{5,197},{6,54},{7,199},{8,56}... | collective-permute-start | bytes 614408 | tf_op jit(solution)/shard_map/ppermute | solution.py:20
  154.2 102.0 %copy-start.13 = (f32[384]{0:T(512)S(1)}, f32[384]{0:T(512)}, u32[]{:S(2)}) copy-start(f32[384]{0:T(512)} %param.75) | copy-start | bytes 4612
  154.2 102.6 %copy-start.6 = (f32[200,384]{1,0:T(8,128)S(1)}, f32[200,384]{1,0:T(8,128)}, u32[]{:S(2)}) copy-start(f32[200,384]{1,0:T(8,128)} %head_ref.1) | copy-start | bytes 921604
  154.2 6.2 %collective-permute-start.80 = (f32[2,200,128]{2,1,0:T(8,128)S(1)}, f32[2,200,128]{2,1,0:T(8,128)S(1)}, u32[]{:S(2)}, u32[]{:S(2)}) collective-permute-start(f32[2,200,128]{2,1,0:T(8,128)S(1)} %get-tuple-element.1145), channel_id=1, source_target_pairs={{0,32},{1,129},{2,34},{3,131},{4,36},{5,133},{6,38},{7,135},{8,40}... | collective-permute-start | bytes 614408 | tf_op jit(solution)/shard_map/ppermute | solution.py:20
  173.0 12.3 %all-to-all-start.1 = ((f32[56,8,128]{2,1,0:T(8,128)}), f32[56,8,128]{2,1,0:T(8,128)S(1)}, u32[]{:S(2)}, u32[]{:S(2)}) async-start(f32[56,8,128]{2,1,0:T(8,128)} %bitcast.10), calls=%async_computation.1 | async-start | bytes 458752 | tf_op jit(solution)/shard_map/all_to_all | solution.py:52
  187.2 7.2 %collective-permute-start.84 = (f32[2,208,128]{2,1,0:T(8,128)S(1)}, f32[2,208,128]{2,1,0:T(8,128)S(1)}, u32[]{:S(2)}, u32[]{:S(2)}) collective-permute-start(f32[2,208,128]{2,1,0:T(8,128)S(1)} %bitcast_bitcast_fusion), channel_id=1, source_target_pairs={{0,48},{1,193},{2,50},{3,195},{4,52},{5,197},{6,54},{7,199},{8,56}... | collective-permute-start | bytes 638984 | tf_op jit(solution)/shard_map/ppermute | solution.py:20
  189.3 6.2 %collective-permute-start.83 = (f32[2,208,128]{2,1,0:T(8,128)S(1)}, f32[2,208,128]{2,1,0:T(8,128)S(1)}, u32[]{:S(2)}, u32[]{:S(2)}) collective-permute-start(f32[2,208,128]{2,1,0:T(8,128)S(1)} %bitcast_bitcast_fusion), channel_id=1, source_target_pairs={{0,32},{1,129},{2,34},{3,131},{4,36},{5,133},{6,38},{7,135},{8,40}... | collective-permute-start | bytes 638984 | tf_op jit(solution)/shard_map/ppermute | solution.py:20
  189.5 6.6 %collective-permute-start.82 = (f32[2,208,128]{2,1,0:T(8,128)S(1)}, f32[2,208,128]{2,1,0:T(8,128)S(1)}, u32[]{:S(2)}, u32[]{:S(2)}) collective-permute-start(f32[2,208,128]{2,1,0:T(8,128)S(1)} %bitcast_bitcast_fusion), channel_id=1, source_target_pairs={{0,16},{1,65},{2,18},{3,67},{4,20},{5,69},{6,22},{7,71},{8,24},{9,... | collective-permute-start | bytes 638984 | tf_op jit(solution)/shard_map/ppermute | solution.py:20
  196.2 24.6 %collective-permute-start.87 = (f32[8,208,128]{2,1,0:T(8,128)S(1)}, f32[8,208,128]{2,1,0:T(8,128)S(1)}, u32[]{:S(2)}, u32[]{:S(2)}) collective-permute-start(f32[8,208,128]{2,1,0:T(8,128)S(1)} %pad_maximum_fusion.1.refs_0_), channel_id=1, source_target_pairs={{0,192},{1,49},{2,194},{3,51},{4,196},{5,53},{6,198},{7,55},{8,200... | collective-permute-start | bytes 2555912 | tf_op jit(solution)/shard_map/ppermute | solution.py:20
  198.7 33.8 %collective-permute-start.86 = (f32[8,208,128]{2,1,0:T(8,128)S(1)}, f32[8,208,128]{2,1,0:T(8,128)S(1)}, u32[]{:S(2)}, u32[]{:S(2)}) collective-permute-start(f32[8,208,128]{2,1,0:T(8,128)S(1)} %pad_maximum_fusion.1.refs_0_), channel_id=1, source_target_pairs={{0,128},{1,33},{2,130},{3,35},{4,132},{5,37},{6,134},{7,39},{8,136... | collective-permute-start | bytes 2555912 | tf_op jit(solution)/shard_map/ppermute | solution.py:20
  198.7 45.6 %collective-permute-start.85 = (f32[8,208,128]{2,1,0:T(8,128)S(1)}, f32[8,208,128]{2,1,0:T(8,128)S(1)}, u32[]{:S(2)}, u32[]{:S(2)}) collective-permute-start(f32[8,208,128]{2,1,0:T(8,128)S(1)} %pad_maximum_fusion.1.refs_0_), channel_id=1, source_target_pairs={{0,64},{1,17},{2,66},{3,19},{4,68},{5,21},{6,70},{7,23},{8,72},{9,... | collective-permute-start | bytes 2555912 | tf_op jit(solution)/shard_map/ppermute | solution.py:20
  199.5 58.1 %collective-permute-start.88 = (f32[8,208,128]{2,1,0:T(8,128)S(1)}, f32[8,208,128]{2,1,0:T(8,128)S(1)}, u32[]{:S(2)}, u32[]{:S(2)}) collective-permute-start(f32[8,208,128]{2,1,0:T(8,128)S(1)} %pad_maximum_fusion.1.refs_0_), channel_id=1, source_target_pairs={{0,1},{1,0},{2,3},{3,2},{4,5},{5,4},{6,7},{7,6},{8,9},{9,8},{10,11... | collective-permute-start | bytes 2555912 | tf_op jit(solution)/shard_map/ppermute | solution.py:20
  220.8 36.8 %collective-permute-start.91 = (f32[8,208,128]{2,1,0:T(8,128)S(1)}, f32[8,208,128]{2,1,0:T(8,128)S(1)}, u32[]{:S(2)}, u32[]{:S(2)}) collective-permute-start(f32[8,208,128]{2,1,0:T(8,128)S(1)} %collective-permute-done.87.refs_3_), channel_id=1, source_target_pairs={{0,1},{1,0},{2,3},{3,2},{4,5},{5,4},{6,7},{7,6},{8,9},{9,8},{10,11... | collective-permute-start | bytes 2555912 | tf_op jit(solution)/shard_map/ppermute | solution.py:20
  232.5 25.1 %collective-permute-start.90 = (f32[8,208,128]{2,1,0:T(8,128)S(1)}, f32[8,208,128]{2,1,0:T(8,128)S(1)}, u32[]{:S(2)}, u32[]{:S(2)}) collective-permute-start(f32[8,208,128]{2,1,0:T(8,128)S(1)} %collective-permute-done.86.refs_2_), channel_id=1, source_target_pairs={{0,1},{1,0},{2,3},{3,2},{4,5},{5,4},{6,7},{7,6},{8,9},{9,8},{10,11... | collective-permute-start | bytes 2555912 | tf_op jit(solution)/shard_map/ppermute | solution.py:20
  244.3 15.9 %collective-permute-start.89 = (f32[8,208,128]{2,1,0:T(8,128)S(1)}, f32[8,208,128]{2,1,0:T(8,128)}, u32[]{:S(2)}, u32[]{:S(2)}) collective-permute-start(f32[8,208,128]{2,1,0:T(8,128)S(1)} %collective-permute-done.85.refs_1_), channel_id=1, source_target_pairs={{0,1},{1,0},{2,3},{3,2},{4,5},{5,4},{6,7},{7,6},{8,9},{9,8},{10,11... | collective-permute-start | bytes 2555912 | tf_op jit(solution)/shard_map/ppermute | solution.py:20
  (12 other events, 168.5 us)
